TPU v7x, 32 devices: a whole 2x2x4 slice. The times are simulated.
32 devices in a mesh: grp: 2 (over x), rows: 4 (over y, core), chan: 4 (over z).
Axes of the slice: x: 2, y: 2, z: 4, core: 2. Of those that a mesh axis runs over, the one named last changes fastest.
Arguments:
- frames_in: bfloat16 [512, 4, 16, 96], P('chan', None, ('grp', 'rows')), parts along dimension 2, may hold values from -48 to 48
- cache_first: bfloat16 [512, 2, 16, 96], P('chan', None, ('grp', 'rows')), parts along dimension 2, may hold values from -6 to 6
- gain_first: float32 [512], P('chan'), may hold values from 0.1 to 1.9
- shift_first: float32 [512], P('chan'), may hold values from -3 to 3
- kernel_first: bfloat16 [3, 3, 3, 512, 512], P(None, None, None, 'chan'), may hold values from -0.0625 to 0.0625
- bias_first: float32 [512], P('chan'), may hold values from -3 to 3
- cache_second: bfloat16 [512, 2, 16, 96], P('chan', None, ('grp', 'rows')), parts along dimension 2, may hold values from -6 to 6
- gain_second: float32 [512], P('chan'), may hold values from 0.1 to 1.9
- shift_second: float32 [512], P('chan'), may hold values from -3 to 3
- kernel_second: bfloat16 [3, 3, 3, 512, 512], P(None, None, None, 'chan'), may hold values from -0.0625 to 0.0625
- bias_second: float32 [512], P('chan'), may hold values from -3 to 3
Outputs:
- decoded: bfloat16 [512, 4, 16, 96], P('chan', None, ('grp', 'rows')), parts along dimension 2
- next_cache: bfloat16 [512, 2, 16, 96], P('chan', None, ('grp', 'rows')), parts along dimension 2
There are 2 independent parts, one for each index of `grp`. A program takes and returns all parts, laid end to end along the dimension named above; an argument that names none is the same for every part. Nothing has to cross between parts.
All inputs are finite; a program needn't handle non-finite values.
Results may differ from a plain program's by a relative error of at most 0.009.
Values may be sent and summed in bfloat16 or wider, within the bound.
A program may use at most 128 MiB of HBM per device.

v0:
```python
import jax
import jax.numpy as jnp
from jax import lax
from jax.sharding import PartitionSpec as P

CHANNELS = 512
GROUPS = 32


def extended(block, sides, width):
    for axis, dim in sides:
        count = lax.axis_size(axis)
        forward = [(i, i + 1) for i in range(count - 1)]
        backward = [(target, source) for source, target in forward]
        low = lax.ppermute(
            lax.slice_in_dim(block, block.shape[dim] - width, None, axis=dim), axis, forward
        )
        high = lax.ppermute(lax.slice_in_dim(block, 0, width, axis=dim), axis, backward)
        block = jnp.concatenate([low, block, high], axis=dim)
    return block


def norm_act(values, gain, shift):
    per_group = CHANNELS // GROUPS
    grouped = values.reshape(values.shape[0] // per_group, -1)
    moments = lax.psum((jnp.sum(grouped, axis=1), jnp.sum(grouped * grouped, axis=1)), "rows")
    entries = grouped.shape[1] * lax.axis_size("rows")
    average = (moments[0] / entries)[:, None]
    squares = (moments[1] / entries)[:, None]
    scaled = ((grouped - average) * lax.rsqrt(squares - average * average + 1e-06)).reshape(
        values.shape
    )
    affine = scaled * gain[:, None, None, None] + shift[:, None, None, None]
    return jax.nn.silu(affine).astype(jnp.bfloat16)


def build_columns(padded, frames):
    widened = jnp.pad(padded, ((0, 0), (0, 0), (0, 0), (1, 1)))
    channel_count = padded.shape[0]
    band_rows = padded.shape[2] - 2
    width_cells = padded.shape[3]
    shifted = [
        widened[:, :, row_tap : row_tap + band_rows, col_tap : col_tap + width_cells]
        for row_tap in range(3)
        for col_tap in range(3)
    ]
    merged = jnp.stack(shifted, 0).reshape(9 * channel_count, frames + 2, band_rows * width_cells)
    return jnp.stack(
        [
            merged[:, time_tap : time_tap + frames].reshape(9 * channel_count, -1)
            for time_tap in range(3)
        ],
        0,
    )


def weight_rows(kernel):
    return kernel.reshape(3, 9 * kernel.shape[3], kernel.shape[4])


def contract(weights, columns):
    running = None
    for time_tap in range(3):
        product = lax.dot_general(
            weights[time_tap],
            columns[time_tap],
            (((0,), (0,)), ((), ())),
            preferred_element_type=jnp.float32,
        )
        running = product if running is None else running + product
    return running


def causal_conv(history, current, kernel, bias):
    joined = jnp.concatenate([history, current], axis=1)
    padded = extended(joined, (("rows", 2),), 1)
    frames = current.shape[1]
    columns = build_columns(padded, frames)
    weights = weight_rows(kernel)
    summed = lax.psum_scatter(contract(weights, columns), "chan", scatter_dimension=0, tiled=True)
    shaped = summed.reshape(current.shape)
    return (shaped + bias[:, None, None, None]).astype(jnp.bfloat16)


def local(
    frames_in,
    cache_first,
    gain_first,
    shift_first,
    kernel_first,
    bias_first,
    cache_second,
    gain_second,
    shift_second,
    kernel_second,
    bias_second,
):
    activated = norm_act(frames_in.astype(jnp.float32), gain_first, shift_first)
    hidden = causal_conv(cache_first, activated, kernel_first, bias_first)
    second = norm_act(hidden.astype(jnp.float32), gain_second, shift_second)
    decoded = causal_conv(cache_second, second, kernel_second, bias_second)
    return (decoded, second[:, second.shape[1] - 2 :])


def solution(mesh):
    return jax.shard_map(
        local,
        mesh=mesh,
        in_specs=(
            P("chan", None, ("grp", "rows"), None),
            P("chan", None, ("grp", "rows"), None),
            P("chan"),
            P("chan"),
            P(None, None, None, "chan", None),
            P("chan"),
            P("chan", None, ("grp", "rows"), None),
            P("chan"),
            P("chan"),
            P(None, None, None, "chan", None),
            P("chan"),
        ),
        out_specs=(P("chan", None, ("grp", "rows"), None), P("chan", None, ("grp", "rows"), None)),
        check_vma=False,
    )
```

profile of v0, /device:TPU:0, one launch (start us, length us, event | category | flops | bytes accessed | tf_op | source)
XLA Modules:
  0.0 196.9 jit_solution(10141624197693270246)
XLA Ops:
  7.2 1.0 convert_reduce_fusion
  8.4 0.1 reduce_sum.51
  8.5 0.1 reduce_sum.54
  8.6 8.4 %all-reduce.3 = (f32[8]{0:T(128)S(1)}, f32[8]{0:T(128)S(1)}) all-reduce(f32[8]{0:T(128)S(1)} %reduce_sum.54, f32[8]{0:T(128)S(1)} %reduce_sum.51), channel_id=1, replica_groups=mesh['grp'=2,'rows'=4,'chan'=4] {'rows'}, use_global_device_ids=true, to_apply=%region_5.6 | all-reduce | flops 16 | bytes 128 | tf_op jit(solution)/shard_map/psum | solution.py:26
  17.3 1.1 fusion.20
  18.4 0.9 fusion.48
  19.3 1.3 collective-permute-start
  20.6 1.4 collective-permute-start.1
  22.1 3.8 %fusion.52 = (bf16[1,3,3,128,512]{4,3,2,1,0:T(8,128)(2,1)}, bf16[1,3,3,128,512]{4,3,2,1,0:T(8,128)(2,1)}, bf16[1,3,3,128,512]{4,3,2,1,0:T(8,128)(2,1)}) fusion(bf16[3,3,3,128,512]{4,3,2,1,0:T(8,128)(2,1)} %param.15), kind=kLoop, calls=%fused_computation.101 | loop fusion | bytes 7077888 | tf_op jit(solution)/shard_map/slice | solution.py:65
  25.9 0.2 fusion.8
  26.7 6.3 %copy.13 = bf16[9,128,6,2,96]{4,3,1,0,2:T(2,128)(2,1)} copy(bf16[9,128,6,2,96]{1,4,3,2,0:T(8,128)(2,1)S(1)} %fusion.36) | data formatting | bytes 5308416 | tf_op jit(solution)/shard_map/stack | solution.py:47
  33.0 6.7 %reshape.65 = bf16[1152,6,192]{2,0,1:T(8,128)(2,1)S(1)} reshape(bf16[9,128,6,2,96]{4,3,1,0,2:T(2,128)(2,1)} %copy.13) | data formatting | bytes 5308416 | tf_op jit(solution)/shard_map/reshape | solution.py:47
  39.7 3.1 %fusion.53 = (bf16[1152,4,192]{2,0,1:T(8,128)(2,1)}, bf16[1152,4,192]{2,0,1:T(8,128)(2,1)}, bf16[1152,4,192]{2,0,1:T(8,128)(2,1)}) fusion(bf16[1152,6,192]{2,0,1:T(8,128)(2,1)S(1)} %reshape.65), kind=kLoop, calls=%fused_computation.102 | loop fusion | bytes 10616832 | tf_op jit(solution)/shard_map/slice | solution.py:50
  42.8 4.2 %copy.16 = bf16[1152,4,192]{0,2,1:T(8,128)(2,1)} copy(bf16[1152,4,192]{2,0,1:T(8,128)(2,1)} %get-tuple-element.19) | data formatting | bytes 3538944 | tf_op jit(solution)/shard_map/slice | solution.py:50
  46.9 4.3 %copy.15 = bf16[1152,4,192]{0,2,1:T(8,128)(2,1)} copy(bf16[1152,4,192]{2,0,1:T(8,128)(2,1)} %get-tuple-element.20) | data formatting | bytes 3538944 | tf_op jit(solution)/shard_map/slice | solution.py:50
  51.2 2.4 %copy.14 = bf16[1152,4,192]{0,2,1:T(8,128)(2,1)} copy(bf16[1152,4,192]{2,0,1:T(8,128)(2,1)S(1)} %copy-done) | data formatting | bytes 3538944 | tf_op jit(solution)/shard_map/slice | solution.py:50
  53.6 2.8 %fusion.55 = f32[768,512]{1,0:T(8,128)S(1)} fusion(bf16[1152,768]{0,1:T(8,128)(2,1)} %bitcast.110, bf16[1152,512]{1,0:T(8,128)(2,1)S(1)} %bitcast.117), kind=kOutput, calls=%fused_computation.104 | convolution fusion | flops 905969664 | bytes 4521984 | tf_op jit(solution)/shard_map/dot_general | solution.py:64
  56.5 1.2 fusion.54
  57.7 0.3 copy-done.4
  57.9 0.3 copy-done.6
  58.3 2.3 %add_bitcast_fusion.1 = f32[512,768]{0,1:T(8,128)} fusion(f32[768,512]{1,0:T(8,128)S(1)} %fusion.54, f32[768,512]{1,0:T(8,128)S(1)} %fusion.55, bf16[1152,768]{0,1:T(8,128)(2,1)S(1)} %bitcast.106, bf16[1152,512]{1,0:T(8,128)(2,1)S(1)} %bitcast.108), kind=kOutput, calls=%fused_computation.3 | convolution fusion | flops 906756096 | bytes 7667712 | tf_op jit(solution)/shard_map/dot_general | solution.py:64
  60.7 38.6 %reduce-scatter.3.cloned.1.call-done = f32[128,768]{0,1:T(8,128)} async-done(((f32[512,768]{0,1:T(8,128)}), f32[128,768]{0,1:T(8,128)}) %reduce-scatter.3.cloned.1.call-update) | async-done | bytes 393232 | tf_op jit(solution)/shard_map/reduce_scatter | solution.py:80
  99.2 1.1 convert_reduce_fusion.1
  100.4 0.1 reduce_sum.72
  100.6 0.1 reduce_sum.75
  100.8 6.9 %all-reduce.2 = (f32[8]{0:T(128)S(1)}, f32[8]{0:T(128)}) all-reduce(f32[8]{0:T(128)S(1)} %reduce_sum.75, f32[8]{0:T(128)S(1)} %reduce_sum.72), channel_id=1, replica_groups=mesh['grp'=2,'rows'=4,'chan'=4] {'rows'}, use_global_device_ids=true, to_apply=%region_12.13 | all-reduce | flops 16 | bytes 128 | tf_op jit(solution)/shard_map/psum | solution.py:26
  107.7 0.7 broadcast_multiply_fusion
  108.6 1.2 multiply_convert_fusion
  109.8 0.9 fusion.46
  110.8 1.3 collective-permute-start.2
  112.1 1.6 collective-permute-start.3
  113.7 1.9 fusion.50
  115.6 1.1 collective-permute-done.3
  116.7 0.2 select_maximum_fusion
  117.5 6.3 %copy.17 = bf16[9,128,6,2,96]{4,3,1,0,2:T(2,128)(2,1)} copy(bf16[9,128,6,2,96]{1,4,3,2,0:T(8,128)(2,1)S(1)} %fusion.26) | data formatting | bytes 5308416 | tf_op jit(solution)/shard_map/stack | solution.py:47
  123.8 6.7 %reshape.67 = bf16[1152,6,192]{2,0,1:T(8,128)(2,1)S(1)} reshape(bf16[9,128,6,2,96]{4,3,1,0,2:T(2,128)(2,1)} %copy.17) | data formatting | bytes 5308416 | tf_op jit(solution)/shard_map/reshape | solution.py:47
  130.5 3.1 %fusion.51 = (bf16[1152,4,192]{2,0,1:T(8,128)(2,1)}, bf16[1152,4,192]{2,0,1:T(8,128)(2,1)}, bf16[1152,4,192]{2,0,1:T(8,128)(2,1)}) fusion(bf16[1152,6,192]{2,0,1:T(8,128)(2,1)S(1)} %reshape.67), kind=kLoop, calls=%fused_computation.100 | loop fusion | bytes 10616832 | tf_op jit(solution)/shard_map/slice | solution.py:50
  133.6 4.2 %copy.20 = bf16[1152,4,192]{0,2,1:T(8,128)(2,1)} copy(bf16[1152,4,192]{2,0,1:T(8,128)(2,1)} %get-tuple-element.13) | data formatting | bytes 3538944 | tf_op jit(solution)/shard_map/slice | solution.py:50
  137.7 4.3 %copy.19 = bf16[1152,4,192]{0,2,1:T(8,128)(2,1)} copy(bf16[1152,4,192]{2,0,1:T(8,128)(2,1)} %get-tuple-element.14) | data formatting | bytes 3538944 | tf_op jit(solution)/shard_map/slice | solution.py:50
  142.0 2.4 %copy.18 = bf16[1152,4,192]{0,2,1:T(8,128)(2,1)} copy(bf16[1152,4,192]{2,0,1:T(8,128)(2,1)S(1)} %copy-done.1) | data formatting | bytes 3538944 | tf_op jit(solution)/shard_map/slice | solution.py:50
  144.5 2.8 %fusion.57 = f32[768,512]{1,0:T(8,128)S(1)} fusion(bf16[1152,768]{0,1:T(8,128)(2,1)} %bitcast.112, bf16[1152,512]{1,0:T(8,128)(2,1)S(1)} %bitcast.118), kind=kOutput, calls=%fused_computation.106 | convolution fusion | flops 905969664 | bytes 4521984 | tf_op jit(solution)/shard_map/dot_general | solution.py:64
  147.3 1.2 fusion.56
  148.5 0.3 copy-done.5
  148.8 0.3 copy-done.7
  149.1 2.3 %add_bitcast_fusion = f32[512,768]{0,1:T(8,128)} fusion(f32[768,512]{1,0:T(8,128)S(1)} %fusion.56, f32[768,512]{1,0:T(8,128)S(1)} %fusion.57, bf16[1152,768]{0,1:T(8,128)(2,1)S(1)} %bitcast.107, bf16[1152,512]{1,0:T(8,128)(2,1)S(1)} %bitcast.109), kind=kOutput, calls=%fused_computation.2 | convolution fusion | flops 906756096 | bytes 7667712 | tf_op jit(solution)/shard_map/dot_general | solution.py:64
  151.5 0.6 slice.176
  152.1 36.2 %reduce-scatter.5.cloned.1.call-done = f32[128,768]{0,1:T(8,128)} async-done(((f32[512,768]{0,1:T(8,128)}), f32[128,768]{0,1:T(8,128)}) %reduce-scatter.5.cloned.1.call-update) | async-done | bytes 393232 | tf_op jit(solution)/shard_map/reduce_scatter | solution.py:80
  188.3 1.7 add_convert_fusion
  (72 shorter events, 2.2 us)
Async XLA Ops:
  7.2 92.1 %reduce-scatter.3.cloned.1.call-start = ((), (), s32[]{:S(2)}) async-start(), calls=%async_computation.2 | async-start | bytes 1966080 | tf_op jit(solution)/shard_map/reduce_scatter | solution.py:80
  19.3 6.6 %collective-permute-start = (bf16[128,6,1,96]{0,3,2,1:T(8,128)(2,1)S(1)}, bf16[128,6,1,96]{0,3,2,1:T(8,128)(2,1)S(1)}, u32[]{:S(2)}, u32[]{:S(2)}) collective-permute-start(bf16[128,6,1,96]{0,3,2,1:T(8,128)(2,1)S(1)} %get-tuple-element.24), channel_id=1, source_target_pairs={{0,4},{4,8},{8,12},{1,5},{5,9},{9,13},{2,6},{6,10},{10,14},{3,7},{... | collective-permute-start | bytes 442376 | tf_op jit(solution)/shard_map/ppermute | solution.py:15
  20.6 5.3 %copy-start.9 = (bf16[128,2,2,96]{0,3,2,1:T(8,128)(2,1)S(1)}, bf16[128,2,2,96]{0,3,2,1:T(8,128)(2,1)}, u32[]{:S(2)}) copy-start(bf16[128,2,2,96]{0,3,2,1:T(8,128)(2,1)} %param.12) | copy-start | bytes 294916
  20.6 5.2 %collective-permute-start.1 = (bf16[128,6,1,96]{0,3,2,1:T(8,128)(2,1)S(1)}, bf16[128,6,1,96]{0,3,2,1:T(8,128)(2,1)S(1)}, u32[]{:S(2)}, u32[]{:S(2)}) collective-permute-start(bf16[128,6,1,96]{0,3,2,1:T(8,128)(2,1)S(1)} %get-tuple-element.25), channel_id=1, source_target_pairs={{4,0},{8,4},{12,8},{5,1},{9,5},{13,9},{6,2},{10,6},{14,10},{7,3},{... | collective-permute-start | bytes 442376 | tf_op jit(solution)/shard_map/ppermute | solution.py:18
  46.9 4.3 %copy-start = (bf16[1152,4,192]{2,0,1:T(8,128)(2,1)S(1)}, bf16[1152,4,192]{2,0,1:T(8,128)(2,1)}, u32[]{:S(2)}) copy-start(bf16[1152,4,192]{2,0,1:T(8,128)(2,1)} %get-tuple-element.21) | copy-start | bytes 5308420
  51.2 2.4 %copy-start.15 = (bf16[1,3,3,128,512]{4,3,2,1,0:T(8,128)(2,1)S(1)}, bf16[1,3,3,128,512]{4,3,2,1,0:T(8,128)(2,1)}, u32[]{:S(2)}) copy-start(bf16[1,3,3,128,512]{4,3,2,1,0:T(8,128)(2,1)} %get-tuple-element.18) | copy-start | bytes 3538948
  53.6 2.8 %copy-start.11 = (bf16[1152,4,192]{0,2,1:T(8,128)(2,1)S(1)}, bf16[1152,4,192]{0,2,1:T(8,128)(2,1)}, u32[]{:S(2)}) copy-start(bf16[1152,4,192]{0,2,1:T(8,128)(2,1)} %copy.14) | copy-start | bytes 5308420
  53.6 2.8 %copy-start.13 = (bf16[1,3,3,128,512]{4,3,2,1,0:T(8,128)(2,1)S(1)}, bf16[1,3,3,128,512]{4,3,2,1,0:T(8,128)(2,1)}, u32[]{:S(2)}) copy-start(bf16[1,3,3,128,512]{4,3,2,1,0:T(8,128)(2,1)} %get-tuple-element.17) | copy-start | bytes 3538948
  56.5 1.5 copy-start.4
  56.5 1.8 copy-start.6
  58.3 41.0 %copy-start.17 = (f32[128]{0:T(128)S(1)}, f32[128]{0:T(128)}, u32[]{:S(2)}) copy-start(f32[128]{0:T(128)} %param.16) | copy-start | bytes 1540
  58.3 55.4 %copy-start.8 = (bf16[3,3,3,128,512]{4,3,2,1,0:T(8,128)(2,1)S(1)}, bf16[3,3,3,128,512]{4,3,2,1,0:T(8,128)(2,1)}, u32[]{:S(2)}) copy-start(bf16[3,3,3,128,512]{4,3,2,1,0:T(8,128)(2,1)} %param.20) | copy-start | bytes 10616836
  60.6 127.7 %reduce-scatter.5.cloned.1.call-start = ((), (), s32[]{:S(2)}) async-start(), calls=%async_computation.3 | async-start | bytes 1966080 | tf_op jit(solution)/shard_map/reduce_scatter | solution.py:80
  109.8 7.5 %copy-start.2 = (bf16[128,4,2,96]{0,3,2,1:T(8,128)(2,1)}, bf16[128,4,2,96]{0,3,2,1:T(8,128)(2,1)S(1)}, u32[]{:S(2)}) copy-start(bf16[128,4,2,96]{0,3,2,1:T(8,128)(2,1)S(1)} %multiply_convert_fusion) | copy-start | bytes 589828
  110.8 4.8 %collective-permute-start.2 = (bf16[128,6,1,96]{0,3,2,1:T(8,128)(2,1)S(1)}, bf16[128,6,1,96]{0,3,2,1:T(8,128)(2,1)S(1)}, u32[]{:S(2)}, u32[]{:S(2)}) collective-permute-start(bf16[128,6,1,96]{0,3,2,1:T(8,128)(2,1)S(1)} %get-tuple-element.22), channel_id=1, source_target_pairs={{0,4},{4,8},{8,12},{1,5},{5,9},{9,13},{2,6},{6,10},{10,14},{3,7},{... | collective-permute-start | bytes 442376 | tf_op jit(solution)/shard_map/ppermute | solution.py:15
  112.1 4.6 %copy-start.10 = (bf16[128,2,2,96]{0,3,2,1:T(8,128)(2,1)S(1)}, bf16[128,2,2,96]{0,3,2,1:T(8,128)(2,1)}, u32[]{:S(2)}) copy-start(bf16[128,2,2,96]{0,3,2,1:T(8,128)(2,1)} %param.17) | copy-start | bytes 294916
  112.1 4.6 %collective-permute-start.3 = (bf16[128,6,1,96]{0,3,2,1:T(8,128)(2,1)S(1)}, bf16[128,6,1,96]{0,3,2,1:T(8,128)(2,1)S(1)}, u32[]{:S(2)}, u32[]{:S(2)}) collective-permute-start(bf16[128,6,1,96]{0,3,2,1:T(8,128)(2,1)S(1)} %get-tuple-element.23), channel_id=1, source_target_pairs={{4,0},{8,4},{12,8},{5,1},{9,5},{13,9},{6,2},{10,6},{14,10},{7,3},{... | collective-permute-start | bytes 442376 | tf_op jit(solution)/shard_map/ppermute | solution.py:18
  137.7 4.3 %copy-start.1 = (bf16[1152,4,192]{2,0,1:T(8,128)(2,1)S(1)}, bf16[1152,4,192]{2,0,1:T(8,128)(2,1)}, u32[]{:S(2)}) copy-start(bf16[1152,4,192]{2,0,1:T(8,128)(2,1)} %get-tuple-element.15) | copy-start | bytes 5308420
  142.0 2.4 %copy-start.16 = (bf16[1,3,3,128,512]{4,3,2,1,0:T(8,128)(2,1)S(1)}, bf16[1,3,3,128,512]{4,3,2,1,0:T(8,128)(2,1)}, u32[]{:S(2)}) copy-start(bf16[1,3,3,128,512]{4,3,2,1,0:T(8,128)(2,1)} %get-tuple-element.12) | copy-start | bytes 3538948
  144.5 2.8 %copy-start.12 = (bf16[1152,4,192]{0,2,1:T(8,128)(2,1)S(1)}, bf16[1152,4,192]{0,2,1:T(8,128)(2,1)}, u32[]{:S(2)}) copy-start(bf16[1152,4,192]{0,2,1:T(8,128)(2,1)} %copy.18) | copy-start | bytes 5308420
  144.5 2.8 %copy-start.14 = (bf16[1,3,3,128,512]{4,3,2,1,0:T(8,128)(2,1)S(1)}, bf16[1,3,3,128,512]{4,3,2,1,0:T(8,128)(2,1)}, u32[]{:S(2)}) copy-start(bf16[1,3,3,128,512]{4,3,2,1,0:T(8,128)(2,1)} %get-tuple-element.11) | copy-start | bytes 3538948
  147.3 1.5 copy-start.5
  147.3 1.8 copy-start.7
  149.1 2.4 %copy-start.3 = (bf16[128,4,2,96]{0,3,2,1:T(8,128)(2,1)S(1)}, bf16[128,4,2,96]{0,3,2,1:T(8,128)(2,1)}, u32[]{:S(2)}) copy-start(bf16[128,4,2,96]{0,3,2,1:T(8,128)(2,1)} %copy-done.2) | copy-start | bytes 589828
  151.4 36.9 %copy-start.18 = (f32[128]{0:T(128)S(1)}, f32[128]{0:T(128)}, u32[]{:S(2)}) copy-start(f32[128]{0:T(128)} %param.21) | copy-start | bytes 1540
Sparse Core Ops, SparseCore 0:
  60.8 38.4 reduce-scatter.2
  151.6 36.7 reduce-scatter.4
where the time goes:
time: 198 us; the launch traced here: 197 us
  waiting for transfers between devices  75.9 us (38%)
  local copies, waits for them, and re-layouts  63.3 us (32%)
  blocking collectives  15.3 us (8%)
  between operations  14.4 us (7%)
  matrix products  12.6 us (6%)
  other arithmetic  9.73 us (5%)
  starting transfers between devices  5.7 us (3%)
    reduce_scatter x2, waiting for transfers between devices, causal_conv(): lax.psum_scatter(contract(weights, columns), 'chan', scatter_dimension=0,...  74.8 us
    slice x8, local copies, waits for them, and re-layouts, build_columns(): merged[:, time_tap:time_tap + frames].reshape(9 * channel_count, -1)  27.9 us
    psum x2, blocking collectives, norm_act(): lax.psum((jnp.sum(grouped, axis=1), jnp.sum(grouped * grouped, axis=1)),...  15.3 us
    reshape x2, local copies, waits for them, and re-layouts, build_columns(): jnp.stack(shifted, 0)  13.4 us
    another operation x4, local copies, waits for them, and re-layouts, build_columns(): jnp.stack(shifted, 0)  12.8 us
    dot_general x6, matrix products, contract(): lax.dot_general(weights[time_tap], columns[time_tap], (((0,), (0,)), ((),...  12.6 us
    slice x2, local copies, waits for them, and re-layouts, contract(): weights[time_tap]  5.66 us
  transfers between devices with their start and end apart: 6, of which 3 were waited for; matrix products, arithmetic and copies ran while one was open for 3% of the time, Pallas kernels for 0%

commit v1 on v0

v1 whole, which is shorter than its diff:
```python
import functools

import jax
import jax.numpy as jnp
from jax import lax
from jax.experimental import pallas as pl
from jax.experimental.pallas import tpu as pltpu
from jax.sharding import PartitionSpec as P

GROUPS = 32
MESH = pl.DeviceIdType.MESH
F32 = jnp.float32
BF16 = jnp.bfloat16


def kernel(
    nr, nc, channels,
    x_hbm, c1_hbm, g1, s1, k1_hbm, b1, c2_hbm, g2, s2, k2_hbm, b2,
    out_ref, next_ref,
    xv, cv, hid, w, x9, halo, mom, part, snd, rcv,
    loc_sem, mom_send, mom_recv, halo_send, halo_recv, rs_send, rs_recv,
):
    frames, band, width, ch = xv.shape
    past = cv.shape[1]
    taps = 9 * ch
    cells = frames * band * width
    r = lax.axis_index("rows")
    c = lax.axis_index("chan")

    loads = [
        pltpu.make_async_copy(src, dst, loc_sem.at[i])
        for i, (src, dst) in enumerate((
            (x_hbm, xv), (c1_hbm, cv.at[0]), (k1_hbm, w.at[0]),
            (c2_hbm, cv.at[1]), (k2_hbm, w.at[1]),
        ))
    ]
    for load in loads:
        load.start()

    barrier = pltpu.get_barrier_semaphore()
    for o in range(1, nr):
        pl.semaphore_signal(
            barrier, inc=1, device_id={"rows": lax.rem(r + o, nr)}, device_id_type=MESH
        )

    @pl.when(c > 0)
    def _():
        pl.semaphore_signal(barrier, inc=1, device_id={"chan": c - 1}, device_id_type=MESH)

    @pl.when(c < nc - 1)
    def _():
        pl.semaphore_signal(barrier, inc=1, device_id={"chan": c + 1}, device_id_type=MESH)

    def moment_copy(conv, o):
        return pltpu.make_async_remote_copy(
            src_ref=mom.at[conv, 0], dst_ref=mom.at[conv, o],
            send_sem=mom_send.at[conv, o], recv_sem=mom_recv.at[conv, o],
            device_id={"rows": lax.rem(r + o, nr)}, device_id_type=MESH,
        )

    def halo_copy(src, conv, kind, side):
        row, step = (band - 1, 1) if side == 0 else (0, nr - 1)
        span = pl.ds(0, past) if kind == 0 else pl.ds(past, frames)
        return pltpu.make_async_remote_copy(
            src_ref=src.at[:, row], dst_ref=halo.at[conv, side, span],
            send_sem=halo_send.at[conv, kind, side], recv_sem=halo_recv.at[conv, kind, side],
            device_id={"rows": lax.rem(r + step, nr)}, device_id_type=MESH,
        )

    def sends_halo(side):
        return r < nr - 1 if side == 0 else r > 0

    def gets_halo(side):
        return r > 0 if side == 0 else r < nr - 1

    def halo_start(src, conv, kind):
        for side in range(2):
            @pl.when(sends_halo(side))
            def _():
                halo_copy(src, conv, kind, side).start()

    def halo_wait(src, conv, kind):
        for side in range(2):
            @pl.when(gets_halo(side))
            def _():
                halo_copy(src, conv, kind, side).wait_recv()

    def halo_drain(src, conv, kind):
        for side in range(2):
            @pl.when(sends_halo(side))
            def _():
                halo_copy(src, conv, kind, side).wait_send()

    def moments(ref, conv):
        v = ref[...].reshape(cells, ch).astype(F32)
        mom[conv, 0] = jnp.concatenate(
            [
                jnp.sum(v, axis=0, keepdims=True),
                jnp.sum(v * v, axis=0, keepdims=True),
                jnp.zeros((6, ch), F32),
            ],
            axis=0,
        )

    def statistics(conv):
        total = mom[conv, 0]
        for o in range(1, nr):
            moment_copy(conv, o).wait_recv()
            total = total + mom[conv, o]
        per_group = channels // GROUPS
        i = lax.broadcasted_iota(jnp.int32, (ch, ch), 0) // per_group
        j = lax.broadcasted_iota(jnp.int32, (ch, ch), 1) // per_group
        same = jnp.where(i == j, 1.0, 0.0).astype(F32)
        total = lax.dot_general(
            total, same, (((1,), (0,)), ((), ())),
            precision=lax.Precision.HIGHEST, preferred_element_type=F32,
        )
        total = total * (1.0 / (per_group * cells * nr))
        average = total[0:1]
        return average, lax.rsqrt(total[1:2] - average * average + 1e-06)

    def place(conv, j, p, v):
        s = lax.broadcasted_iota(jnp.int32, (width, ch), 0)
        low = jnp.where(s == 0, 0.0, pltpu.roll(v, 1, 0))
        high = jnp.where(s == width - 1, 0.0, pltpu.roll(v, width - 1, 0))
        for ds, t in enumerate((low, v, high)):
            t = t.astype(BF16)
            for dr in range(3):
                if 0 <= p - dr < band:
                    first = (dr * 3 + ds) * ch
                    x9[conv, j, p - dr, :, first : first + ch] = t

    def row_of(src, conv, j, f, p):
        if p == 0:
            return halo[conv, 0, j]
        if p == band + 1:
            return halo[conv, 1, j]
        return src[f, p - 1]

    def inside(p, v):
        if p == 0:
            return jnp.where(r > 0, v, jnp.zeros_like(v))
        if p == band + 1:
            return jnp.where(r < nr - 1, v, jnp.zeros_like(v))
        return v

    def place_past(conv):
        def body(f, _):
            for p in range(band + 2):
                v = row_of(cv.at[conv], conv, f, f, p).astype(F32)
                place(conv, f, p, inside(p, v))
            return 0

        lax.fori_loop(0, past, body, 0)

    def place_current(src, conv, gain, shift, stats, keep=None):
        average, inverse = stats
        gain, shift = gain[...], shift[...]

        def body(f, _):
            for p in range(band + 2):
                v = row_of(src, conv, f + past, f, p).astype(F32)
                u = ((v - average) * inverse) * gain + shift
                v = (u / (1.0 + jnp.exp(-u))).astype(BF16)
                if keep is not None and 1 <= p <= band:
                    hid[f, p - 1] = v
                place(conv, f + past, p, inside(p, v.astype(F32)))
            return 0

        lax.fori_loop(0, frames, body, 0)

    gw = max(256, ch)
    ngroups = (nc * ch) // gw
    each = gw // ch
    fb = 2 if frames % 2 == 0 else 1
    mb = fb * band * width

    def multiply(conv, g):
        cols = pl.ds(pl.multiple_of(g * gw, gw), gw)

        def body(m, _):
            acc = None
            for dt in range(3):
                lhs = x9[conv, pl.ds(m * fb + dt, fb)].reshape(mb, taps)
                prod = jnp.dot(
                    lhs, w[conv, dt * taps : (dt + 1) * taps, cols], preferred_element_type=F32
                )
                acc = prod if acc is None else acc + prod
            rows = pl.ds(pl.multiple_of(m * mb, mb), mb)
            for q in range(each):
                part[g * each + q, rows] = acc[:, q * ch : (q + 1) * ch]
            return 0

        lax.fori_loop(0, frames // fb, body, 0)

    def rs_copy(conv, d, way):
        return pltpu.make_async_remote_copy(
            src_ref=snd.at[conv, d], dst_ref=rcv.at[conv, way, d],
            send_sem=rs_send.at[conv, d], recv_sem=rs_recv.at[conv, way, d],
            device_id={"chan": c + 1 - 2 * way}, device_id_type=MESH,
        )

    def first_send(conv, d, way):
        snd[conv, d] = part[d].astype(BF16)
        rs_copy(conv, d, way).start()

    def pass_on(conv, d, way):
        rs_copy(conv, d, way).wait_recv()
        snd[conv, d] = (part[d] + rcv[conv, way, d].astype(F32)).astype(BF16)
        rs_copy(conv, d, way).start()

    def convolve(conv, bias, meanwhile=None):
        start = jnp.where(c < nc // 2, ngroups // 2, 0)
        far = [(d, 0) for d in range(nc - 1, nc // 2 - 1, -1)]
        near = [(d, 0) for d in range(nc // 2 - 1, 0, -1)]
        far_left = [(d, 1) for d in range(nc // 2)]
        near_left = [(d, 1) for d in range(nc // 2, nc - 1)]
        for i in range(ngroups):
            multiply(conv, lax.rem(start + i, ngroups))
            if i == max(ngroups // 2, 1) - 1:
                @pl.when(c == 0)
                def _():
                    for d, way in far:
                        first_send(conv, d, way)

                @pl.when(c == nc - 1)
                def _():
                    for d, way in far_left:
                        first_send(conv, d, way)

        @pl.when(c == 0)
        def _():
            for d, way in near:
                first_send(conv, d, way)

        @pl.when(c == nc - 1)
        def _():
            for d, way in near_left:
                first_send(conv, d, way)

        if meanwhile is not None:
            meanwhile()

        for (d, _), (e, _) in zip(far + near, far_left + near_left):
            @pl.when((c > 0) & (c < d))
            def _():
                pass_on(conv, d, 0)

            @pl.when((c < nc - 1) & (c > e))
            def _():
                pass_on(conv, e, 1)

        for way, condition in ((0, c > 0), (1, c < nc - 1)):
            @pl.when(condition)
            def _():
                rs_copy(conv, c, way).wait_recv()
                part[c] = part[c] + rcv[conv, way, c].astype(F32)

        return (part[c] + bias[...]).astype(BF16).reshape(frames, band, width, ch)

    loads[0].wait()
    moments(xv, 0)
    pl.semaphore_wait(
        barrier, nr - 1 + jnp.where(c > 0, 1, 0) + jnp.where(c < nc - 1, 1, 0)
    )
    for o in range(1, nr):
        moment_copy(0, o).start()
    halo_start(xv, 0, 1)
    loads[1].wait()
    halo_start(cv.at[0], 0, 0)
    loads[3].wait()
    halo_start(cv.at[1], 1, 0)

    halo_wait(cv.at[0], 0, 0)
    place_past(0)
    halo_wait(xv, 0, 1)
    place_current(xv, 0, g1, s1, statistics(0))
    loads[2].wait()

    def early():
        halo_wait(cv.at[1], 1, 0)
        place_past(1)

    halo_drain(xv, 0, 1)
    xv[...] = convolve(0, b1, early)
    moments(xv, 1)
    for o in range(1, nr):
        moment_copy(1, o).start()
    halo_start(xv, 1, 1)
    halo_wait(xv, 1, 1)
    place_current(xv, 1, g2, s2, statistics(1), keep=True)
    next_ref[...] = hid[frames - past : frames]
    loads[4].wait()
    out_ref[...] = convolve(1, b2)

    halo_drain(cv.at[0], 0, 0)
    halo_drain(cv.at[1], 1, 0)
    halo_drain(xv, 1, 1)
    for conv in range(2):
        for o in range(1, nr):
            moment_copy(conv, o).wait_send()
        for d in range(nc):
            @pl.when(c < d)
            def _():
                rs_copy(conv, d, 0).wait_send()

            @pl.when(c > d)
            def _():
                rs_copy(conv, d, 1).wait_send()


def local(nr, nc, frames_in, cache_first, gain_first, shift_first, kernel_first, bias_first,
          cache_second, gain_second, shift_second, kernel_second, bias_second):
    def inner(a):
        return jnp.transpose(a, (1, 2, 3, 0))

    ch, frames, band, width = frames_in.shape
    past = cache_first.shape[1]
    channels = kernel_first.shape[4]
    depth = 27 * ch
    hbm = pl.BlockSpec(memory_space=pl.ANY)
    vmem = pl.BlockSpec(memory_space=pltpu.VMEM)
    cells = frames * band * width
    decoded, kept = pl.pallas_call(
        functools.partial(kernel, nr, nc, channels),
        out_shape=(
            jax.ShapeDtypeStruct((frames, band, width, ch), BF16),
            jax.ShapeDtypeStruct((past, band, width, ch), BF16),
        ),
        in_specs=[hbm, hbm, vmem, vmem, hbm, vmem, hbm, vmem, vmem, hbm, vmem],
        out_specs=(vmem, vmem),
        scratch_shapes=[
            pltpu.VMEM((frames, band, width, ch), BF16),
            pltpu.VMEM((2, past, band, width, ch), BF16),
            pltpu.VMEM((frames, band, width, ch), BF16),
            pltpu.VMEM((2, depth, channels), BF16),
            pltpu.VMEM((2, past + frames, band, width, 9 * ch), BF16),
            pltpu.VMEM((2, 2, past + frames, width, ch), BF16),
            pltpu.VMEM((2, nr, 8, ch), F32),
            pltpu.VMEM((nc, cells, ch), F32),
            pltpu.VMEM((2, nc, cells, ch), BF16),
            pltpu.VMEM((2, 2, nc, cells, ch), BF16),
            pltpu.SemaphoreType.DMA((5,)),
            pltpu.SemaphoreType.DMA((2, nr)),
            pltpu.SemaphoreType.DMA((2, nr)),
            pltpu.SemaphoreType.DMA((2, 2, 2)),
            pltpu.SemaphoreType.DMA((2, 2, 2)),
            pltpu.SemaphoreType.DMA((2, nc)),
            pltpu.SemaphoreType.DMA((2, 2, nc)),
        ],
        compiler_params=pltpu.CompilerParams(
            collective_id=0, has_side_effects=True, vmem_limit_bytes=50 * 1024 * 1024
        ),
        cost_estimate=pl.CostEstimate(
            flops=4 * cells * depth * channels, bytes_accessed=4 * depth * channels, transcendentals=0
        ),
    )(
        inner(frames_in), inner(cache_first), gain_first[None], shift_first[None],
        kernel_first.reshape(depth, channels), bias_first[None],
        inner(cache_second), gain_second[None], shift_second[None],
        kernel_second.reshape(depth, channels), bias_second[None],
    )
    return jnp.transpose(decoded, (3, 0, 1, 2)), jnp.transpose(kept, (3, 0, 1, 2))


def solution(mesh):
    tile = P("chan", None, ("grp", "rows"), None)
    taps = P(None, None, None, "chan", None)
    return jax.shard_map(
        functools.partial(local, mesh.shape["rows"], mesh.shape["chan"]),
        mesh=mesh,
        in_specs=(
            tile, tile, P("chan"), P("chan"), taps, P("chan"),
            tile, P("chan"), P("chan"), taps, P("chan"),
        ),
        out_specs=(tile, tile),
        check_vma=False,
    )
```

time: 198 us -> 69.3 us (0.35)
  waiting for transfers between devices: 75.9 us -> 0 us
  Pallas kernels: 0 us -> 60.5 us
  local copies, waits for them, and re-layouts: 63.3 us -> 7.95 us
  blocking collectives: 15.3 us -> 0 us
  between operations: 14.4 us -> 0.66 us
  matrix products: 12.6 us -> 0 us
  other arithmetic: 9.73 us -> 0 us
  starting transfers between devices: 5.7 us -> 0 us
    reduce_scatter x2 -> x0, waiting for transfers between devices: 74.8 us -> none  [causal_conv(): lax.psum_scatter(contract(weights, columns), 'chan', scatter_dimension=0,...]
    pallas_call x0 -> x1, Pallas kernels: none -> 60.5 us  [local(): pl.pallas_call(functools.partial(kernel, nr, nc, channels), out_shape=(ja...]
    slice x11 -> x0, local copies, waits for them, and re-layouts: 34.2 us -> none  [the longest x8 27.9 us: build_columns(): merged[:, time_tap:time_tap + frames].reshape(9 * channel_count, -1)]
    psum x2 -> x0, blocking collectives: 15.3 us -> none  [norm_act(): lax.psum((jnp.sum(grouped, axis=1), jnp.sum(grouped * grouped, axis=1)),...]
    reshape x2 -> x0, local copies, waits for them, and re-layouts: 13.4 us -> none  [build_columns(): jnp.stack(shifted, 0)]
    another operation x4 -> x0, local copies, waits for them, and re-layouts: 12.8 us -> none  [build_columns(): jnp.stack(shifted, 0)]
    dot_general x6 -> x0, matrix products: 12.6 us -> none  [contract(): lax.dot_general(weights[time_tap], columns[time_tap], (((0,), (0,)), ((),...]
    unnamed x48 -> x20, local copies, waits for them, and re-layouts: 1.92 us -> 7.95 us
  transfers between devices with their start and end apart: 6 -> 0, of which waited for: 3 -> 0; matrix products, arithmetic and copies ran while one was open for 3% -> 0% of each run, Pallas kernels for 0% -> 0%
where the time goes in v1:
time: 69.3 us; the launch traced here: 69.1 us
  Pallas kernels  60.5 us (87%)
  local copies, waits for them, and re-layouts  7.95 us (11%)
    pallas_call x1, Pallas kernels, local(): pl.pallas_call(functools.partial(kernel, nr, nc, channels), out_shape=(ja...  60.5 us
    unnamed x20, local copies, waits for them, and re-layouts  7.95 us

profile of v1, /device:TPU:0, one launch (start us, length us, event | category | flops | bytes accessed | tf_op | source)
XLA Modules:
  0.0 69.1 jit_solution(15922856092407965507)
XLA Ops:
  0.6 0.0 copy-start
  0.6 0.9 %copy-done = bf16[128,4,2,96]{0,3,2,1:T(8,128)(2,1)S(1)} copy-done((bf16[128,4,2,96]{0,3,2,1:T(8,128)(2,1)S(1)}, bf16[128,4,2,96]{0,3,2,1:T(8,128)(2,1)}, u32[]{:S(2)}) %copy-start) | copy-done | bytes 196632
  1.6 0.0 copy-start.1
  1.6 0.9 %copy-done.1 = bf16[128,2,2,96]{0,3,2,1:T(8,128)(2,1)S(1)} copy-done((bf16[128,2,2,96]{0,3,2,1:T(8,128)(2,1)S(1)}, bf16[128,2,2,96]{0,3,2,1:T(8,128)(2,1)}, u32[]{:S(2)}) %copy-start.1) | copy-done | bytes 98328
  2.5 0.0 copy-start.2
  2.5 0.9 %copy-done.2 = bf16[128,2,2,96]{0,3,2,1:T(8,128)(2,1)S(1)} copy-done((bf16[128,2,2,96]{0,3,2,1:T(8,128)(2,1)S(1)}, bf16[128,2,2,96]{0,3,2,1:T(8,128)(2,1)}, u32[]{:S(2)}) %copy-start.2) | copy-done | bytes 98328
  3.3 0.0 copy-start.3
  3.4 0.7 copy-done.3
  4.0 0.0 copy-start.4
  4.0 0.7 copy-done.4
  4.7 0.0 copy-start.5
  4.7 0.7 copy-done.5
  5.3 0.0 copy-start.6
  5.3 0.7 copy-done.6
  6.0 0.0 copy-start.7
  6.0 0.7 copy-done.7
  6.6 0.0 copy-start.8
  6.6 0.7 copy-done.8
  7.3 60.5 %shard_map.122 = (bf16[4,2,96,128]{3,2,1,0:T(8,128)(2,1)S(1)}, bf16[2,2,96,128]{3,2,1,0:T(8,128)(2,1)S(1)}) custom-call(bf16[4,2,96,128]{3,2,1,0:T(8,128)(2,1)S(1)} %bitcast.15, bf16[2,2,96,128]{3,2,1,0:T(8,128)(2,1)S(1)} %bitcast.16, f32[1,128]{1,0:T(1,128)S(1)} %bitcast.18, f32[1,128]{1,0:T(1,128)S(1)} %bitcast.19, bf16[3456,512]{1,0:T(8,128)(2,1)} %bitcast.24, ...), custom_call_target="tpu_custom_call" | custom-call | flops 5435817984 | bytes 7077888 | tf_op jit(solution)/shard_map/pallas_call | solution.py:324
  67.8 0.7 copy.15
  68.4 0.6 copy.16
Async XLA Ops:
  0.6 0.9 %copy-start = (bf16[128,4,2,96]{0,3,2,1:T(8,128)(2,1)S(1)}, bf16[128,4,2,96]{0,3,2,1:T(8,128)(2,1)}, u32[]{:S(2)}) copy-start(bf16[128,4,2,96]{0,3,2,1:T(8,128)(2,1)} %param.11) | copy-start | bytes 589828
  1.6 0.9 %copy-start.1 = (bf16[128,2,2,96]{0,3,2,1:T(8,128)(2,1)S(1)}, bf16[128,2,2,96]{0,3,2,1:T(8,128)(2,1)}, u32[]{:S(2)}) copy-start(bf16[128,2,2,96]{0,3,2,1:T(8,128)(2,1)} %param.12) | copy-start | bytes 294916
  2.5 0.9 %copy-start.2 = (bf16[128,2,2,96]{0,3,2,1:T(8,128)(2,1)S(1)}, bf16[128,2,2,96]{0,3,2,1:T(8,128)(2,1)}, u32[]{:S(2)}) copy-start(bf16[128,2,2,96]{0,3,2,1:T(8,128)(2,1)} %param.17) | copy-start | bytes 294916
  3.3 0.7 copy-start.3
  4.0 0.7 copy-start.4
  4.7 0.7 copy-start.5
  5.3 0.7 copy-start.6
  6.0 0.7 copy-start.7
  6.6 0.7 copy-start.8

commit v2 on v1

v2 whole, which is shorter than its diff:
```python
import functools

import jax
import jax.numpy as jnp
from jax import lax
from jax.experimental import pallas as pl
from jax.experimental.pallas import tpu as pltpu
from jax.sharding import PartitionSpec as P

GROUPS = 32
MESH = pl.DeviceIdType.MESH
F32 = jnp.float32
BF16 = jnp.bfloat16


def kernel(
    nr, nc, channels,
    x_hbm, c1_hbm, g1_hbm, s1_hbm, k1_hbm, b1_hbm, c2_hbm, g2_hbm, s2_hbm, k2_hbm, b2_hbm,
    out_ref, next_ref,
    xv, cv, vecs, w, x9, halo, mom, part, snd, rcv,
    loc_sem, mom_send, mom_recv, halo_send, halo_recv, rs_send, rs_recv,
):
    frames, band, width, ch = xv.shape
    past = cv.shape[1]
    taps = 9 * ch
    cells = frames * band * width
    r = lax.axis_index("rows")
    c = lax.axis_index("chan")

    loads = [
        pltpu.make_async_copy(src, dst, loc_sem.at[i])
        for i, (src, dst) in enumerate((
            (x_hbm, xv), (c1_hbm, cv.at[0]), (k1_hbm, w.at[0]),
            (c2_hbm, cv.at[1]), (k2_hbm, w.at[1]),
            (g1_hbm, vecs.at[0]), (s1_hbm, vecs.at[1]), (b1_hbm, vecs.at[2]),
            (g2_hbm, vecs.at[3]), (s2_hbm, vecs.at[4]), (b2_hbm, vecs.at[5]),
        ))
    ]
    for load in loads:
        load.start()

    barrier = pltpu.get_barrier_semaphore()
    for o in range(1, nr):
        pl.semaphore_signal(
            barrier, inc=1, device_id={"rows": lax.rem(r + o, nr)}, device_id_type=MESH
        )

    @pl.when(c > 0)
    def _():
        pl.semaphore_signal(barrier, inc=1, device_id={"chan": c - 1}, device_id_type=MESH)

    @pl.when(c < nc - 1)
    def _():
        pl.semaphore_signal(barrier, inc=1, device_id={"chan": c + 1}, device_id_type=MESH)

    def moment_copy(conv, o):
        return pltpu.make_async_remote_copy(
            src_ref=mom.at[conv, 0], dst_ref=mom.at[conv, o],
            send_sem=mom_send.at[conv, o], recv_sem=mom_recv.at[conv, o],
            device_id={"rows": lax.rem(r + o, nr)}, device_id_type=MESH,
        )

    def halo_copy(src, conv, kind, side):
        row, step = (band - 1, 1) if side == 0 else (0, nr - 1)
        span = pl.ds(0, past) if kind == 0 else pl.ds(past, frames)
        return pltpu.make_async_remote_copy(
            src_ref=src.at[:, row], dst_ref=halo.at[conv, side, span],
            send_sem=halo_send.at[conv, kind, side], recv_sem=halo_recv.at[conv, kind, side],
            device_id={"rows": lax.rem(r + step, nr)}, device_id_type=MESH,
        )

    def sends_halo(side):
        return r < nr - 1 if side == 0 else r > 0

    def gets_halo(side):
        return r > 0 if side == 0 else r < nr - 1

    def halo_start(src, conv, kind):
        for side in range(2):
            @pl.when(sends_halo(side))
            def _():
                halo_copy(src, conv, kind, side).start()

    def halo_wait(src, conv, kind):
        for side in range(2):
            @pl.when(gets_halo(side))
            def _():
                halo_copy(src, conv, kind, side).wait_recv()

    def halo_drain(src, conv, kind):
        for side in range(2):
            @pl.when(sends_halo(side))
            def _():
                halo_copy(src, conv, kind, side).wait_send()

    def sums_of(v):
        v = v.astype(F32)
        return jnp.sum(v, axis=0, keepdims=True), jnp.sum(v * v, axis=0, keepdims=True)

    def set_moments(conv, sums):
        mom[conv, 0] = jnp.concatenate([*sums, jnp.zeros((6, ch), F32)], axis=0)

    def statistics(conv):
        total = mom[conv, 0]
        for o in range(1, nr):
            moment_copy(conv, o).wait_recv()
            total = total + mom[conv, o]
        per_group = channels // GROUPS
        i = lax.broadcasted_iota(jnp.int32, (ch, ch), 0) // per_group
        j = lax.broadcasted_iota(jnp.int32, (ch, ch), 1) // per_group
        same = jnp.where(i == j, 1.0, 0.0).astype(BF16)
        high = total.astype(BF16)
        rest = total - high.astype(F32)
        middle = rest.astype(BF16)
        low = (rest - middle.astype(F32)).astype(BF16)
        thirds = jnp.concatenate([t.astype(F32) for t in (high, middle, low)], axis=0)
        thirds = jnp.dot(thirds.astype(BF16), same, preferred_element_type=F32)
        total = (thirds[16:24] + thirds[8:16]) + thirds[0:8]
        total = total * (1.0 / (per_group * cells * nr))
        average = total[0:1]
        return average, lax.rsqrt(total[1:2] - average * average + 1e-06)

    def place(conv, j, p, v):
        s = lax.broadcasted_iota(jnp.int32, (width, ch), 0)
        low = jnp.where(s == 0, 0.0, pltpu.roll(v, 1, 0))
        high = jnp.where(s == width - 1, 0.0, pltpu.roll(v, width - 1, 0))
        for ds, t in enumerate((low, v, high)):
            t = t.astype(BF16)
            for dr in range(3):
                if 0 <= p - dr < band:
                    first = (dr * 3 + ds) * ch
                    x9[conv, j, p - dr, :, first : first + ch] = t

    def row_of(src, conv, j, f, p):
        if p == 0:
            return halo[conv, 0, j]
        if p == band + 1:
            return halo[conv, 1, j]
        return src[f, p - 1]

    def inside(p, v):
        if p == 0:
            return jnp.where(r > 0, v, jnp.zeros_like(v))
        if p == band + 1:
            return jnp.where(r < nr - 1, v, jnp.zeros_like(v))
        return v

    def place_past(conv):
        def body(f, _):
            for p in range(band + 2):
                v = row_of(cv.at[conv], conv, f, f, p).astype(F32)
                place(conv, f, p, inside(p, v))
            return 0

        lax.fori_loop(0, past, body, 0)

    def place_current(src, conv, gain, shift, stats, sides, keep=False):
        average, inverse = stats
        gain, shift = vecs[gain], vecs[shift]

        def body(f, _):
            for p in sides:
                v = row_of(src, conv, f + past, f, p).astype(F32)
                u = ((v - average) * inverse) * gain + shift
                v = (u / (1.0 + jnp.exp(-u))).astype(BF16)
                if keep:
                    @pl.when(f >= frames - past)
                    def _():
                        next_ref[f - (frames - past), p - 1] = v
                place(conv, f + past, p, inside(p, v.astype(F32)))
            return 0

        lax.fori_loop(0, frames, body, 0)

    own, edges = range(1, band + 1), (0, band + 1)
    gw = max(256, ch)
    ngroups = (nc * ch) // gw
    each = gw // ch
    fb = 2 if frames % 2 == 0 else 1
    mb = fb * band * width

    piece = band * width

    def multiply(conv, g, m):
        cols = pl.ds(pl.multiple_of(g * gw, gw), gw)
        acc = None
        for dt in range(3):
            lhs = x9[conv, pl.ds(m * fb + dt, fb)].reshape(mb, taps)
            prod = jnp.dot(
                lhs, w[conv, dt * taps : (dt + 1) * taps, cols], preferred_element_type=F32
            )
            acc = prod if acc is None else acc + prod
        rows = pl.ds(pl.multiple_of(m * mb, mb), mb)
        for q in range(each):
            part[g * each + q, rows] = acc[:, q * ch : (q + 1) * ch]

    def rs_copy(conv, d, m, way):
        return pltpu.make_async_remote_copy(
            src_ref=snd.at[conv, d, m], dst_ref=rcv.at[conv, way, d, m],
            send_sem=rs_send.at[conv, d, m], recv_sem=rs_recv.at[conv, way, d, m],
            device_id={"chan": c + 1 - 2 * way}, device_id_type=MESH,
        )

    def rows_of(m):
        return pl.ds(pl.multiple_of(m * piece, piece), piece)

    def first_send(conv, d, way, start, count):
        def body(i, _):
            m = start + i
            snd[conv, d, m] = part[d, rows_of(m)].astype(BF16)
            rs_copy(conv, d, m, way).start()
            return 0

        lax.fori_loop(0, count, body, 0)

    def pass_on(conv, d, way):
        def body(m, _):
            rs_copy(conv, d, m, way).wait_recv()
            total = part[d, rows_of(m)] + rcv[conv, way, d, m].astype(F32)
            snd[conv, d, m] = total.astype(BF16)
            rs_copy(conv, d, m, way).start()
            return 0

        lax.fori_loop(0, frames, body, 0)

    def convolve(conv, bias, dst, meanwhile=None):
        start = jnp.where(c < nc // 2, ngroups // 2, 0)
        half = max(ngroups // 2, 1)
        right = [(d, 0) for d in range(nc - 1, 0, -1)]
        left = [(d, 1) for d in range(nc - 1)]
        blocks = frames // fb

        def steps(first, count):
            def body(i, _):
                g = lax.rem(start + first + i // blocks, ngroups)
                m = lax.rem(i, blocks)
                multiply(conv, g, m)
                if first == 0:
                    @pl.when((c == 0) & (i >= (half - 1) * blocks))
                    def _():
                        first_send(conv, nc - 1, 0, m * fb, fb)

                    @pl.when((c == nc - 1) & (i >= (half - 1) * blocks))
                    def _():
                        first_send(conv, 0, 1, m * fb, fb)
                return 0

            lax.fori_loop(0, count * blocks, body, 0)

        def ends(low, high):
            @pl.when(c == 0)
            def _():
                for d, way in right[low:high]:
                    first_send(conv, d, way, 0, frames)

            @pl.when(c == nc - 1)
            def _():
                for d, way in left[low:high]:
                    first_send(conv, d, way, 0, frames)

        steps(0, half)
        ends(1, nc // 2)
        if ngroups > half:
            steps(half, ngroups - half)
        ends(max(nc // 2, 1), nc - 1)
        if meanwhile is not None:
            meanwhile()

        def relay(near, far):
            for (d, way), (e, yaw) in zip(near, far):
                for chunk, to in ((d, way), (e, yaw)):
                    beyond = (c > 0) & (c < chunk) if to == 0 else (c < nc - 1) & (c > chunk)

                    @pl.when(beyond)
                    def _():
                        pass_on(conv, chunk, to)

        @pl.when(c < nc // 2)
        def _():
            relay(right, left)

        @pl.when(c >= nc // 2)
        def _():
            relay(left, right)

        def body(m, sums):
            for way, condition in ((0, c > 0), (1, c < nc - 1)):
                @pl.when(condition)
                def _():
                    rs_copy(conv, c, m, way).wait_recv()
                    part[c, rows_of(m)] = part[c, rows_of(m)] + rcv[conv, way, c, m].astype(F32)
            v = (part[c, rows_of(m)] + vecs[bias]).astype(BF16)
            dst[m] = v.reshape(band, width, ch)
            more = sums_of(v)
            return sums[0] + more[0], sums[1] + more[1]

        zero = jnp.zeros((1, ch), F32)
        return lax.fori_loop(0, frames, body, (zero, zero))

    loads[0].wait()
    set_moments(0, sums_of(xv[...].reshape(cells, ch)))
    pl.semaphore_wait(
        barrier, nr - 1 + jnp.where(c > 0, 1, 0) + jnp.where(c < nc - 1, 1, 0)
    )
    for o in range(1, nr):
        moment_copy(0, o).start()
    halo_start(xv, 0, 1)
    loads[1].wait()
    halo_start(cv.at[0], 0, 0)
    loads[3].wait()
    halo_start(cv.at[1], 1, 0)

    halo_wait(cv.at[0], 0, 0)
    place_past(0)
    for load in loads[5:]:
        load.wait()
    stats = statistics(0)
    place_current(xv, 0, 0, 1, stats, own)
    halo_wait(xv, 0, 1)
    place_current(xv, 0, 0, 1, stats, edges)
    loads[2].wait()
    halo_drain(xv, 0, 1)

    def early():
        halo_wait(cv.at[1], 1, 0)
        place_past(1)

    set_moments(1, convolve(0, 2, xv, early))
    for o in range(1, nr):
        moment_copy(1, o).start()
    halo_start(xv, 1, 1)
    stats = statistics(1)
    place_current(xv, 1, 3, 4, stats, own, keep=True)
    halo_wait(xv, 1, 1)
    place_current(xv, 1, 3, 4, stats, edges)
    loads[4].wait()
    convolve(1, 5, out_ref)

    halo_drain(cv.at[0], 0, 0)
    halo_drain(cv.at[1], 1, 0)
    halo_drain(xv, 1, 1)
    for conv in range(2):
        for o in range(1, nr):
            moment_copy(conv, o).wait_send()
        for d in range(nc):
            for way, condition in ((0, c < d), (1, c > d)):
                @pl.when(condition)
                def _():
                    def body(m, _):
                        rs_copy(conv, d, m, way).wait_send()
                        return 0

                    lax.fori_loop(0, frames, body, 0)


def local(nr, nc, frames_in, cache_first, gain_first, shift_first, kernel_first, bias_first,
          cache_second, gain_second, shift_second, kernel_second, bias_second):
    def inner(a):
        return jnp.transpose(a, (1, 2, 3, 0))

    ch, frames, band, width = frames_in.shape
    past = cache_first.shape[1]
    channels = kernel_first.shape[4]
    depth = 27 * ch
    hbm = pl.BlockSpec(memory_space=pltpu.HBM)
    vmem = pl.BlockSpec(memory_space=pltpu.VMEM)
    cells = frames * band * width
    decoded, kept = pl.pallas_call(
        functools.partial(kernel, nr, nc, channels),
        out_shape=(
            jax.ShapeDtypeStruct((frames, band, width, ch), BF16),
            jax.ShapeDtypeStruct((past, band, width, ch), BF16),
        ),
        in_specs=[hbm] * 11,
        out_specs=(vmem, vmem),
        scratch_shapes=[
            pltpu.VMEM((frames, band, width, ch), BF16),
            pltpu.VMEM((2, past, band, width, ch), BF16),
            pltpu.VMEM((6, 1, ch), F32),
            pltpu.VMEM((2, depth, channels), BF16),
            pltpu.VMEM((2, past + frames, band, width, 9 * ch), BF16),
            pltpu.VMEM((2, 2, past + frames, width, ch), BF16),
            pltpu.VMEM((2, nr, 8, ch), F32),
            pltpu.VMEM((nc, cells, ch), F32),
            pltpu.VMEM((2, nc, frames, band * width, ch), BF16),
            pltpu.VMEM((2, 2, nc, frames, band * width, ch), BF16),
            pltpu.SemaphoreType.DMA((11,)),
            pltpu.SemaphoreType.DMA((2, nr)),
            pltpu.SemaphoreType.DMA((2, nr)),
            pltpu.SemaphoreType.DMA((2, 2, 2)),
            pltpu.SemaphoreType.DMA((2, 2, 2)),
            pltpu.SemaphoreType.DMA((2, nc, frames)),
            pltpu.SemaphoreType.DMA((2, 2, nc, frames)),
        ],
        compiler_params=pltpu.CompilerParams(
            collective_id=0, has_side_effects=True, vmem_limit_bytes=63 * 1024 * 1024
        ),
        cost_estimate=pl.CostEstimate(
            flops=4 * cells * depth * channels, bytes_accessed=4 * depth * channels, transcendentals=0
        ),
    )(
        inner(frames_in), inner(cache_first), gain_first[None], shift_first[None],
        kernel_first.reshape(depth, channels), bias_first[None],
        inner(cache_second), gain_second[None], shift_second[None],
        kernel_second.reshape(depth, channels), bias_second[None],
    )
    return jnp.transpose(decoded, (3, 0, 1, 2)), jnp.transpose(kept, (3, 0, 1, 2))


def solution(mesh):
    tile = P("chan", None, ("grp", "rows"), None)
    taps = P(None, None, None, "chan", None)
    return jax.shard_map(
        functools.partial(local, mesh.shape["rows"], mesh.shape["chan"]),
        mesh=mesh,
        in_specs=(
            tile, tile, P("chan"), P("chan"), taps, P("chan"),
            tile, P("chan"), P("chan"), taps, P("chan"),
        ),
        out_specs=(tile, tile),
        check_vma=False,
    )
```

time: 69.3 us -> 49.2 us (0.71)
  Pallas kernels: 60.5 us -> 44.7 us
  local copies, waits for them, and re-layouts: 7.95 us -> 3.16 us
    pallas_call x1, Pallas kernels: 60.5 us -> 44.7 us  [local(): pl.pallas_call(functools.partial(kernel, nr, nc, channels), out_shape=(ja...]
    unnamed x20 -> x2, local copies, waits for them, and re-layouts: 7.95 us -> 3.16 us
where the time goes in v2:
time: 49.2 us; the launch traced here: 48.5 us
  Pallas kernels  44.7 us (91%)
  local copies, waits for them, and re-layouts  3.16 us (6%)
  between operations  0.64 us (1%)
    pallas_call x1, Pallas kernels, local(): pl.pallas_call(functools.partial(kernel, nr, nc, channels), out_shape=(ja...  44.7 us
    unnamed x2, local copies, waits for them, and re-layouts  3.16 us

profile of v2, /device:TPU:0, one launch (start us, length us, event | category | flops | bytes accessed | tf_op | source)
XLA Modules:
  0.0 48.5 jit_solution(8665038465790977106)
XLA Ops:
  0.6 44.7 %shard_map.122 = (bf16[4,2,96,128]{3,2,1,0:T(8,128)(2,1)}, bf16[2,2,96,128]{3,2,1,0:T(8,128)(2,1)}) custom-call(bf16[4,2,96,128]{3,2,1,0:T(8,128)(2,1)} %bitcast.17, bf16[2,2,96,128]{3,2,1,0:T(8,128)(2,1)} %bitcast.18, f32[1,128]{1,0:T(1,128)} %bitcast.20, f32[1,128]{1,0:T(1,128)} %bitcast.21, bf16[3456,512]{1,0:T(8,128)(2,1)} %bitcast.15, ...), custom_call_target="tpu_custom_call" | custom-call | flops 5435817984 | bytes 7077888 | tf_op jit(solution)/shard_map/pallas_call | solution.py:368
  45.4 1.6 %copy.15 = bf16[128,4,2,96]{0,3,2,1:T(8,128)(2,1)} copy(bf16[128,4,2,96]{0,3,2,1:T(8,128)(2,1)} %bitcast.13) | data formatting | bytes 393216
  47.0 1.5 %copy.16 = bf16[128,2,2,96]{0,3,2,1:T(8,128)(2,1)} copy(bf16[128,2,2,96]{0,3,2,1:T(8,128)(2,1)} %bitcast.14) | data formatting | bytes 196608

commit v3 on v2

--- a/solution.py
+++ b/solution.py
@@ -16,14 +16,15 @@
 def kernel(
     nr, nc, channels,
     x_hbm, c1_hbm, g1_hbm, s1_hbm, k1_hbm, b1_hbm, c2_hbm, g2_hbm, s2_hbm, k2_hbm, b2_hbm,
-    out_ref, next_ref,
-    xv, cv, vecs, w, x9, halo, mom, part, snd, rcv,
-    loc_sem, mom_send, mom_recv, halo_send, halo_recv, rs_send, rs_recv,
+    out_hbm, next_hbm,
+    xv, cv, vecs, kept, w, x9, halo, mom, part, snd, rcv,
+    loc_sem, out_sem, mom_send, mom_recv, halo_send, halo_recv, rs_send, rs_recv,
 ):
     frames, band, width, ch = xv.shape
     past = cv.shape[1]
     taps = 9 * ch
     cells = frames * band * width
+    fb = 2 if frames % 2 == 0 else 1
     r = lax.axis_index("rows")
     c = lax.axis_index("chan")
 
@@ -36,9 +37,6 @@
             (g2_hbm, vecs.at[3]), (s2_hbm, vecs.at[4]), (b2_hbm, vecs.at[5]),
         ))
     ]
-    for load in loads:
-        load.start()
-
     barrier = pltpu.get_barrier_semaphore()
     for o in range(1, nr):
         pl.semaphore_signal(
@@ -52,6 +50,9 @@
     @pl.when(c < nc - 1)
     def _():
         pl.semaphore_signal(barrier, inc=1, device_id={"chan": c + 1}, device_id_type=MESH)
+
+    for i in (0, 1, 3, *range(5, len(loads))):
+        loads[i].start()
 
     def moment_copy(conv, o):
         return pltpu.make_async_remote_copy(
@@ -154,7 +155,7 @@
 
         lax.fori_loop(0, past, body, 0)
 
-    def place_current(src, conv, gain, shift, stats, sides, keep=False):
+    def place_current(src, conv, gain, shift, stats, sides, first, keep=False):
         average, inverse = stats
         gain, shift = vecs[gain], vecs[shift]
 
@@ -166,17 +167,16 @@
                 if keep:
                     @pl.when(f >= frames - past)
                     def _():
-                        next_ref[f - (frames - past), p - 1] = v
+                        kept[f - (frames - past), p - 1] = v
                 place(conv, f + past, p, inside(p, v.astype(F32)))
             return 0
 
-        lax.fori_loop(0, frames, body, 0)
+        lax.fori_loop(first, first + fb, body, 0)
 
     own, edges = range(1, band + 1), (0, band + 1)
     gw = max(256, ch)
     ngroups = (nc * ch) // gw
     each = gw // ch
-    fb = 2 if frames % 2 == 0 else 1
     mb = fb * band * width
 
     piece = band * width
@@ -223,17 +223,33 @@
 
         lax.fori_loop(0, frames, body, 0)
 
-    def convolve(conv, bias, dst, meanwhile=None):
+    def convolve(conv, bias, prepare, finish, meanwhile=None):
         start = jnp.where(c < nc // 2, ngroups // 2, 0)
         half = max(ngroups // 2, 1)
         right = [(d, 0) for d in range(nc - 1, 0, -1)]
         left = [(d, 1) for d in range(nc - 1)]
         blocks = frames // fb
 
+        def ends(low, high):
+            @pl.when(c == 0)
+            def _():
+                for d, way in right[low:high]:
+                    first_send(conv, d, way, 0, frames)
+
+            @pl.when(c == nc - 1)
+            def _():
+                for d, way in left[low:high]:
+                    first_send(conv, d, way, 0, frames)
+
         def steps(first, count):
             def body(i, _):
                 g = lax.rem(start + first + i // blocks, ngroups)
                 m = lax.rem(i, blocks)
+                if first == 0:
+                    if half == 1:
+                        prepare(m)
+                    else:
+                        pl.when(i < blocks)(lambda: prepare(m))
                 multiply(conv, g, m)
                 if first == 0:
                     @pl.when((c == 0) & (i >= (half - 1) * blocks))
@@ -243,25 +259,17 @@
                     @pl.when((c == nc - 1) & (i >= (half - 1) * blocks))
                     def _():
                         first_send(conv, 0, 1, m * fb, fb)
+                else:
+                    pl.when(i == 0)(lambda: ends(1, nc // 2))
                 return 0
 
             lax.fori_loop(0, count * blocks, body, 0)
 
-        def ends(low, high):
-            @pl.when(c == 0)
-            def _():
-                for d, way in right[low:high]:
-                    first_send(conv, d, way, 0, frames)
-
-            @pl.when(c == nc - 1)
-            def _():
-                for d, way in left[low:high]:
-                    first_send(conv, d, way, 0, frames)
-
         steps(0, half)
-        ends(1, nc // 2)
         if ngroups > half:
             steps(half, ngroups - half)
+        else:
+            ends(1, nc // 2)
         ends(max(nc // 2, 1), nc - 1)
         if meanwhile is not None:
             meanwhile()
@@ -290,14 +298,33 @@
                     rs_copy(conv, c, m, way).wait_recv()
                     part[c, rows_of(m)] = part[c, rows_of(m)] + rcv[conv, way, c, m].astype(F32)
             v = (part[c, rows_of(m)] + vecs[bias]).astype(BF16)
-            dst[m] = v.reshape(band, width, ch)
+            xv[m] = v.reshape(band, width, ch)
+            finish(m)
             more = sums_of(v)
             return sums[0] + more[0], sums[1] + more[1]
 
         zero = jnp.zeros((1, ch), F32)
         return lax.fori_loop(0, frames, body, (zero, zero))
 
+    def prepare(conv, gain, shift, stats, keep):
+        def body(m):
+            @pl.when(m > 0)
+            def _():
+                place_current(xv, conv, gain, shift, stats, own, m * fb, keep)
+
+            place_current(xv, conv, gain, shift, stats, edges, m * fb)
+
+        place_current(xv, conv, gain, shift, stats, own, 0, keep)
+        halo_wait(xv, conv, 1)
+        return body
+
+    def out_copy(f):
+        return pltpu.make_async_copy(xv.at[f], out_hbm.at[f], out_sem.at[f])
+
+    next_copy = pltpu.make_async_copy(kept, next_hbm, out_sem.at[frames])
+
     loads[0].wait()
+    loads[2].start()
     set_moments(0, sums_of(xv[...].reshape(cells, ch)))
     pl.semaphore_wait(
         barrier, nr - 1 + jnp.where(c > 0, 1, 0) + jnp.where(c < nc - 1, 1, 0)
@@ -309,36 +336,38 @@
     halo_start(cv.at[0], 0, 0)
     loads[3].wait()
     halo_start(cv.at[1], 1, 0)
+    loads[4].start()
 
     halo_wait(cv.at[0], 0, 0)
     place_past(0)
     for load in loads[5:]:
         load.wait()
-    stats = statistics(0)
-    place_current(xv, 0, 0, 1, stats, own)
-    halo_wait(xv, 0, 1)
-    place_current(xv, 0, 0, 1, stats, edges)
+    ready = prepare(0, 0, 1, statistics(0), False)
     loads[2].wait()
-    halo_drain(xv, 0, 1)
 
     def early():
         halo_wait(cv.at[1], 1, 0)
         place_past(1)
-
-    set_moments(1, convolve(0, 2, xv, early))
+        halo_drain(xv, 0, 1)
+
+    set_moments(1, convolve(0, 2, ready, lambda m: None, early))
     for o in range(1, nr):
         moment_copy(1, o).start()
     halo_start(xv, 1, 1)
-    stats = statistics(1)
-    place_current(xv, 1, 3, 4, stats, own, keep=True)
-    halo_wait(xv, 1, 1)
-    place_current(xv, 1, 3, 4, stats, edges)
+    ready = prepare(1, 3, 4, statistics(1), True)
     loads[4].wait()
-    convolve(1, 5, out_ref)
+
+    def saved():
+        next_copy.start()
+        halo_drain(xv, 1, 1)
+
+    convolve(1, 5, ready, lambda m: out_copy(m).start(), saved)
+    for f in range(frames):
+        out_copy(f).wait()
+    next_copy.wait()
 
     halo_drain(cv.at[0], 0, 0)
     halo_drain(cv.at[1], 1, 0)
-    halo_drain(xv, 1, 1)
     for conv in range(2):
         for o in range(1, nr):
             moment_copy(conv, o).wait_send()
@@ -353,6 +382,17 @@
                     lax.fori_loop(0, frames, body, 0)
 
 
+def hand_over(a_hbm, b_hbm, c_hbm, d_hbm, sems):
+    copies = []
+    for src, dst in ((a_hbm, c_hbm), (b_hbm, d_hbm)):
+        for f in range(src.shape[0]):
+            copies.append(pltpu.make_async_copy(src.at[f], dst.at[f], sems.at[len(copies)]))
+    for copy in copies:
+        copy.start()
+    for copy in copies:
+        copy.wait()
+
+
 def local(nr, nc, frames_in, cache_first, gain_first, shift_first, kernel_first, bias_first,
           cache_second, gain_second, shift_second, kernel_second, bias_second):
     def inner(a):
@@ -363,7 +403,6 @@
     channels = kernel_first.shape[4]
     depth = 27 * ch
     hbm = pl.BlockSpec(memory_space=pltpu.HBM)
-    vmem = pl.BlockSpec(memory_space=pltpu.VMEM)
     cells = frames * band * width
     decoded, kept = pl.pallas_call(
         functools.partial(kernel, nr, nc, channels),
@@ -372,11 +411,12 @@
             jax.ShapeDtypeStruct((past, band, width, ch), BF16),
         ),
         in_specs=[hbm] * 11,
-        out_specs=(vmem, vmem),
+        out_specs=(hbm, hbm),
         scratch_shapes=[
             pltpu.VMEM((frames, band, width, ch), BF16),
             pltpu.VMEM((2, past, band, width, ch), BF16),
             pltpu.VMEM((6, 1, ch), F32),
+            pltpu.VMEM((past, band, width, ch), BF16),
             pltpu.VMEM((2, depth, channels), BF16),
             pltpu.VMEM((2, past + frames, band, width, 9 * ch), BF16),
             pltpu.VMEM((2, 2, past + frames, width, ch), BF16),
@@ -385,6 +425,7 @@
             pltpu.VMEM((2, nc, frames, band * width, ch), BF16),
             pltpu.VMEM((2, 2, nc, frames, band * width, ch), BF16),
             pltpu.SemaphoreType.DMA((11,)),
+            pltpu.SemaphoreType.DMA((frames + 1,)),
             pltpu.SemaphoreType.DMA((2, nr)),
             pltpu.SemaphoreType.DMA((2, nr)),
             pltpu.SemaphoreType.DMA((2, 2, 2)),
@@ -404,6 +445,16 @@
         inner(cache_second), gain_second[None], shift_second[None],
         kernel_second.reshape(depth, channels), bias_second[None],
     )
+    decoded, kept = pl.pallas_call(
+        hand_over,
+        out_shape=(
+            jax.ShapeDtypeStruct(decoded.shape, BF16), jax.ShapeDtypeStruct(kept.shape, BF16),
+        ),
+        in_specs=[hbm, hbm],
+        out_specs=(hbm, hbm),
+        scratch_shapes=[pltpu.SemaphoreType.DMA((frames + past,))],
+        compiler_params=pltpu.CompilerParams(vmem_limit_bytes=63 * 1024 * 1024),
+    )(decoded, kept)
     return jnp.transpose(decoded, (3, 0, 1, 2)), jnp.transpose(kept, (3, 0, 1, 2))
 
 

time: 49.2 us -> 55.7 us (1.13)
  Pallas kernels: 44.7 us -> 54.5 us
  local copies, waits for them, and re-layouts: 3.16 us -> 0 us
    pallas_call x0 -> x1, Pallas kernels: none -> 10.1 us  [local(): pl.pallas_call(hand_over, out_shape=(jax.ShapeDtypeStruct(decoded.shape,...]
    unnamed x2 -> x0, local copies, waits for them, and re-layouts: 3.16 us -> none
where the time goes in v3:
time: 55.7 us; the launch traced here: 55.1 us
  Pallas kernels  54.5 us (98%)
  between operations  0.64 us (1%)
    pallas_call x1, Pallas kernels, local(): pl.pallas_call(functools.partial(kernel, nr, nc, channels), out_shape=(ja...  44.4 us
    pallas_call x1, Pallas kernels, local(): pl.pallas_call(hand_over, out_shape=(jax.ShapeDtypeStruct(decoded.shape,...  10.1 us

profile of v3, /device:TPU:0, one launch (start us, length us, event | category | flops | bytes accessed | tf_op | source)
XLA Modules:
  0.0 55.1 jit_solution(11693371821394696238)
XLA Ops:
  0.6 44.4 %shard_map.122 = (bf16[4,2,96,128]{3,2,1,0:T(8,128)(2,1)}, bf16[2,2,96,128]{3,2,1,0:T(8,128)(2,1)}) custom-call(bf16[4,2,96,128]{3,2,1,0:T(8,128)(2,1)} %bitcast.15, bf16[2,2,96,128]{3,2,1,0:T(8,128)(2,1)} %bitcast.17, f32[1,128]{1,0:T(1,128)} %bitcast.20, f32[1,128]{1,0:T(1,128)} %bitcast.21, bf16[3456,512]{1,0:T(8,128)(2,1)} %bitcast.13, ...), custom_call_target="tpu_custom_call" | custom-call | flops 5435817984 | bytes 7077888 | tf_op jit(solution)/shard_map/pallas_call | solution.py:407
  45.0 10.1 %shard_map.123 = (bf16[4,2,96,128]{3,2,1,0:T(8,128)(2,1)}, bf16[2,2,96,128]{3,2,1,0:T(8,128)(2,1)}) custom-call(bf16[4,2,96,128]{3,2,1,0:T(8,128)(2,1)} %get-tuple-element.6.a_hbm, bf16[2,2,96,128]{3,2,1,0:T(8,128)(2,1)} %get-tuple-element.7.b_hbm), custom_call_target="tpu_custom_call" | custom-call | tf_op jit(solution)/shard_map/pallas_call | solution.py:448

commit v4 on v3

--- a/solution.py
+++ b/solution.py
@@ -146,9 +146,9 @@
             return jnp.where(r < nr - 1, v, jnp.zeros_like(v))
         return v
 
-    def place_past(conv):
+    def place_past(conv, sides):
         def body(f, _):
-            for p in range(band + 2):
+            for p in sides:
                 v = row_of(cv.at[conv], conv, f, f, p).astype(F32)
                 place(conv, f, p, inside(p, v))
             return 0
@@ -213,17 +213,18 @@
 
         lax.fori_loop(0, count, body, 0)
 
-    def pass_on(conv, d, way):
-        def body(m, _):
+    def pass_on(conv, d, way, start, count):
+        def body(i, _):
+            m = start + i
             rs_copy(conv, d, m, way).wait_recv()
             total = part[d, rows_of(m)] + rcv[conv, way, d, m].astype(F32)
             snd[conv, d, m] = total.astype(BF16)
             rs_copy(conv, d, m, way).start()
             return 0
 
-        lax.fori_loop(0, frames, body, 0)
-
-    def convolve(conv, bias, prepare, finish, meanwhile=None):
+        lax.fori_loop(0, count, body, 0)
+
+    def convolve(conv, bias, prepare, finish, meanwhile):
         start = jnp.where(c < nc // 2, ngroups // 2, 0)
         half = max(ngroups // 2, 1)
         right = [(d, 0) for d in range(nc - 1, 0, -1)]
@@ -261,6 +262,14 @@
                         first_send(conv, 0, 1, m * fb, fb)
                 else:
                     pl.when(i == 0)(lambda: ends(1, nc // 2))
+
+                    @pl.when((i < blocks) & (c > 0) & (c < nc // 2))
+                    def _():
+                        pass_on(conv, nc - 1, 0, i * fb, fb)
+
+                    @pl.when((i < blocks) & (c >= nc // 2) & (c < nc - 1))
+                    def _():
+                        pass_on(conv, 0, 1, i * fb, fb)
                 return 0
 
             lax.fori_loop(0, count * blocks, body, 0)
@@ -271,25 +280,26 @@
         else:
             ends(1, nc // 2)
         ends(max(nc // 2, 1), nc - 1)
-        if meanwhile is not None:
-            meanwhile()
-
-        def relay(near, far):
-            for (d, way), (e, yaw) in zip(near, far):
-                for chunk, to in ((d, way), (e, yaw)):
-                    beyond = (c > 0) & (c < chunk) if to == 0 else (c < nc - 1) & (c > chunk)
-
-                    @pl.when(beyond)
-                    def _():
-                        pass_on(conv, chunk, to)
+
+        def relay(order):
+            for d, way in order:
+                beyond = (c > 0) & (c < d) if way == 0 else (c < nc - 1) & (c > d)
+
+                @pl.when(beyond)
+                def _():
+                    pass_on(conv, d, way, 0, frames)
+
+        done = 1 if ngroups > half else 0
 
         @pl.when(c < nc // 2)
         def _():
-            relay(right, left)
+            relay(right[:1 - done] + [x for pair in zip(left, right[1:]) for x in pair] + left[-1:])
 
         @pl.when(c >= nc // 2)
         def _():
-            relay(left, right)
+            relay(left[:1 - done] + [x for pair in zip(right, left[1:]) for x in pair] + right[-1:])
+
+        meanwhile()
 
         def body(m, sums):
             for way, condition in ((0, c > 0), (1, c < nc - 1)):
@@ -316,6 +326,9 @@
 
         place_current(xv, conv, gain, shift, stats, own, 0, keep)
         halo_wait(xv, conv, 1)
+        if conv == 0:
+            halo_wait(cv.at[0], 0, 0)
+            place_past(0, edges)
         return body
 
     def out_copy(f):
@@ -334,20 +347,18 @@
     halo_start(xv, 0, 1)
     loads[1].wait()
     halo_start(cv.at[0], 0, 0)
+    place_past(0, own)
+    for load in loads[5:]:
+        load.wait()
+    ready = prepare(0, 0, 1, statistics(0), False)
     loads[3].wait()
     halo_start(cv.at[1], 1, 0)
     loads[4].start()
-
-    halo_wait(cv.at[0], 0, 0)
-    place_past(0)
-    for load in loads[5:]:
-        load.wait()
-    ready = prepare(0, 0, 1, statistics(0), False)
     loads[2].wait()
 
     def early():
         halo_wait(cv.at[1], 1, 0)
-        place_past(1)
+        place_past(1, range(band + 2))
         halo_drain(xv, 0, 1)
 
     set_moments(1, convolve(0, 2, ready, lambda m: None, early))
@@ -382,15 +393,22 @@
                     lax.fori_loop(0, frames, body, 0)
 
 
-def hand_over(a_hbm, b_hbm, c_hbm, d_hbm, sems):
+def hand_over(a_hbm, b_hbm, c_hbm, d_hbm, a_held, b_held, in_sem, out_sem):
     copies = []
-    for src, dst in ((a_hbm, c_hbm), (b_hbm, d_hbm)):
+    for src, held, dst in ((a_hbm, a_held, c_hbm), (b_hbm, b_held, d_hbm)):
         for f in range(src.shape[0]):
-            copies.append(pltpu.make_async_copy(src.at[f], dst.at[f], sems.at[len(copies)]))
-    for copy in copies:
-        copy.start()
-    for copy in copies:
-        copy.wait()
+            i = len(copies)
+            copies.append((
+                pltpu.make_async_copy(src.at[f], held.at[f], in_sem.at[i]),
+                pltpu.make_async_copy(held.at[f], dst.at[f], out_sem.at[i]),
+            ))
+    for arrive, _ in copies:
+        arrive.start()
+    for arrive, leave in copies:
+        arrive.wait()
+        leave.start()
+    for _, leave in copies:
+        leave.wait()
 
 
 def local(nr, nc, frames_in, cache_first, gain_first, shift_first, kernel_first, bias_first,
@@ -452,7 +470,10 @@
         ),
         in_specs=[hbm, hbm],
         out_specs=(hbm, hbm),
-        scratch_shapes=[pltpu.SemaphoreType.DMA((frames + past,))],
+        scratch_shapes=[
+            pltpu.VMEM(decoded.shape, BF16), pltpu.VMEM(kept.shape, BF16),
+            pltpu.SemaphoreType.DMA((frames + past,)), pltpu.SemaphoreType.DMA((frames + past,)),
+        ],
         compiler_params=pltpu.CompilerParams(vmem_limit_bytes=63 * 1024 * 1024),
     )(decoded, kept)
     return jnp.transpose(decoded, (3, 0, 1, 2)), jnp.transpose(kept, (3, 0, 1, 2))

time: 55.7 us -> 45.8 us (0.82)
  Pallas kernels: 54.5 us -> 44.5 us
    pallas_call x1, Pallas kernels: 10.1 us -> 1.64 us  [local(): pl.pallas_call(hand_over, out_shape=(jax.ShapeDtypeStruct(decoded.shape,...]
    pallas_call x1, Pallas kernels: 44.4 us -> 42.9 us  [local(): pl.pallas_call(functools.partial(kernel, nr, nc, channels), out_shape=(ja...]
where the time goes in v4:
time: 45.8 us; the launch traced here: 45.2 us
  Pallas kernels  44.5 us (97%)
  between operations  0.64 us (1%)
    pallas_call x1, Pallas kernels, local(): pl.pallas_call(functools.partial(kernel, nr, nc, channels), out_shape=(ja...  42.9 us
    pallas_call x1, Pallas kernels, local(): pl.pallas_call(hand_over, out_shape=(jax.ShapeDtypeStruct(decoded.shape,...  1.64 us

profile of v4, /device:TPU:0, one launch (start us, length us, event | category | flops | bytes accessed | tf_op | source)
XLA Modules:
  0.0 45.2 jit_solution(10610559989034746266)
XLA Ops:
  0.6 42.9 %shard_map.122 = (bf16[4,2,96,128]{3,2,1,0:T(8,128)(2,1)}, bf16[2,2,96,128]{3,2,1,0:T(8,128)(2,1)}) custom-call(bf16[4,2,96,128]{3,2,1,0:T(8,128)(2,1)} %bitcast.15, bf16[2,2,96,128]{3,2,1,0:T(8,128)(2,1)} %bitcast.17, f32[1,128]{1,0:T(1,128)} %bitcast.20, f32[1,128]{1,0:T(1,128)} %bitcast.21, bf16[3456,512]{1,0:T(8,128)(2,1)} %bitcast.13, ...), custom_call_target="tpu_custom_call" | custom-call | flops 5435817984 | bytes 7077888 | tf_op jit(solution)/shard_map/pallas_call | solution.py:425
  43.5 1.6 %shard_map.123 = (bf16[4,2,96,128]{3,2,1,0:T(8,128)(2,1)}, bf16[2,2,96,128]{3,2,1,0:T(8,128)(2,1)}) custom-call(bf16[4,2,96,128]{3,2,1,0:T(8,128)(2,1)} %get-tuple-element.6.a_hbm, bf16[2,2,96,128]{3,2,1,0:T(8,128)(2,1)} %get-tuple-element.7.b_hbm), custom_call_target="tpu_custom_call" | custom-call | tf_op jit(solution)/shard_map/pallas_call | solution.py:466

commit v5 on v4

--- a/solution.py
+++ b/solution.py
@@ -27,6 +27,15 @@
     fb = 2 if frames % 2 == 0 else 1
     r = lax.axis_index("rows")
     c = lax.axis_index("chan")
+    half_line = nc // 2
+    side = c // half_line
+    inner = 1 - 2 * side
+    place_in = c * (1 - side) + (nc - 1 - c) * side
+    border = (place_in + 1) // half_line
+
+    def chunk_at(d):
+        return d * (1 - side) + (nc - 1 - d) * side
+
 
     loads = [
         pltpu.make_async_copy(src, dst, loc_sem.at[i])
@@ -50,6 +59,19 @@
     @pl.when(c < nc - 1)
     def _():
         pl.semaphore_signal(barrier, inc=1, device_id={"chan": c + 1}, device_id_type=MESH)
+
+    @pl.when(border == 0)
+    def _():
+        pl.semaphore_signal(
+            barrier, inc=1, device_id={"chan": chunk_at(half_line)}, device_id_type=MESH
+        )
+
+    for d in range(half_line + 1, nc):
+        @pl.when(border == 1)
+        def _():
+            pl.semaphore_signal(
+                barrier, inc=1, device_id={"chan": chunk_at(d)}, device_id_type=MESH
+            )
 
     for i in (0, 1, 3, *range(5, len(loads))):
         loads[i].start()
@@ -194,119 +216,95 @@
         for q in range(each):
             part[g * each + q, rows] = acc[:, q * ch : (q + 1) * ch]
 
-    def rs_copy(conv, d, m, way):
+    def rs_copy(conv, d, m, way, target):
         return pltpu.make_async_remote_copy(
             src_ref=snd.at[conv, d, m], dst_ref=rcv.at[conv, way, d, m],
             send_sem=rs_send.at[conv, d, m], recv_sem=rs_recv.at[conv, way, d, m],
-            device_id={"chan": c + 1 - 2 * way}, device_id_type=MESH,
+            device_id={"chan": target}, device_id_type=MESH,
         )
+
+    def sent_copy(conv, d, m, inward):
+        if inward:
+            target = border * d + (1 - border) * (c + inner)
+            return rs_copy(conv, d, m, 2 * border, target)
+        return rs_copy(conv, d, m, 1, c - inner)
 
     def rows_of(m):
         return pl.ds(pl.multiple_of(m * piece, piece), piece)
 
-    def first_send(conv, d, way, start, count):
+    def take(conv, d, m, way):
+        rs_copy(conv, d, m, way, lax.rem(c + 1, nc)).wait_recv()
+        part[d, rows_of(m)] = part[d, rows_of(m)] + rcv[conv, way, d, m].astype(F32)
+
+    def emit(conv, spot, inward, start, count):
+        d = chunk_at(spot)
+        way, adds = (0, place_in > 0) if inward else (1, border == 0)
+
         def body(i, _):
             m = start + i
+
+            @pl.when(adds)
+            def _():
+                take(conv, d, m, way)
+
             snd[conv, d, m] = part[d, rows_of(m)].astype(BF16)
-            rs_copy(conv, d, m, way).start()
+            sent_copy(conv, d, m, inward).start()
             return 0
 
         lax.fori_loop(0, count, body, 0)
 
-    def pass_on(conv, d, way, start, count):
-        def body(i, _):
-            m = start + i
-            rs_copy(conv, d, m, way).wait_recv()
-            total = part[d, rows_of(m)] + rcv[conv, way, d, m].astype(F32)
-            snd[conv, d, m] = total.astype(BF16)
-            rs_copy(conv, d, m, way).start()
+    def convolve(conv, bias, prepare, finish, meanwhile):
+        start = (1 - side) * (ngroups // 2)
+        half = ngroups // 2
+        blocks = frames // fb
+
+        def far_block(i, _):
+            m = lax.rem(i, blocks)
+            pl.when(i < blocks)(lambda: prepare(m))
+            multiply(conv, lax.rem(start + i // blocks, ngroups), m)
+
+            @pl.when((place_in == 0) & (i >= (half - 1) * blocks))
+            def _():
+                emit(conv, nc - 1, True, m * fb, fb)
+
             return 0
 
-        lax.fori_loop(0, count, body, 0)
-
-    def convolve(conv, bias, prepare, finish, meanwhile):
-        start = jnp.where(c < nc // 2, ngroups // 2, 0)
-        half = max(ngroups // 2, 1)
-        right = [(d, 0) for d in range(nc - 1, 0, -1)]
-        left = [(d, 1) for d in range(nc - 1)]
-        blocks = frames // fb
-
-        def ends(low, high):
-            @pl.when(c == 0)
-            def _():
-                for d, way in right[low:high]:
-                    first_send(conv, d, way, 0, frames)
-
-            @pl.when(c == nc - 1)
-            def _():
-                for d, way in left[low:high]:
-                    first_send(conv, d, way, 0, frames)
-
-        def steps(first, count):
-            def body(i, _):
-                g = lax.rem(start + first + i // blocks, ngroups)
-                m = lax.rem(i, blocks)
-                if first == 0:
-                    if half == 1:
-                        prepare(m)
-                    else:
-                        pl.when(i < blocks)(lambda: prepare(m))
-                multiply(conv, g, m)
-                if first == 0:
-                    @pl.when((c == 0) & (i >= (half - 1) * blocks))
-                    def _():
-                        first_send(conv, nc - 1, 0, m * fb, fb)
-
-                    @pl.when((c == nc - 1) & (i >= (half - 1) * blocks))
-                    def _():
-                        first_send(conv, 0, 1, m * fb, fb)
-                else:
-                    pl.when(i == 0)(lambda: ends(1, nc // 2))
-
-                    @pl.when((i < blocks) & (c > 0) & (c < nc // 2))
-                    def _():
-                        pass_on(conv, nc - 1, 0, i * fb, fb)
-
-                    @pl.when((i < blocks) & (c >= nc // 2) & (c < nc - 1))
-                    def _():
-                        pass_on(conv, 0, 1, i * fb, fb)
-                return 0
-
-            lax.fori_loop(0, count * blocks, body, 0)
-
-        steps(0, half)
-        if ngroups > half:
-            steps(half, ngroups - half)
-        else:
-            ends(1, nc // 2)
-        ends(max(nc // 2, 1), nc - 1)
-
-        def relay(order):
-            for d, way in order:
-                beyond = (c > 0) & (c < d) if way == 0 else (c < nc - 1) & (c > d)
-
-                @pl.when(beyond)
-                def _():
-                    pass_on(conv, d, way, 0, frames)
-
-        done = 1 if ngroups > half else 0
-
-        @pl.when(c < nc // 2)
-        def _():
-            relay(right[:1 - done] + [x for pair in zip(left, right[1:]) for x in pair] + left[-1:])
-
-        @pl.when(c >= nc // 2)
-        def _():
-            relay(left[:1 - done] + [x for pair in zip(right, left[1:]) for x in pair] + right[-1:])
+        def near_block(i, _):
+            multiply(conv, lax.rem(start + half + i // blocks, ngroups), lax.rem(i, blocks))
+
+            @pl.when((i == 0) & (place_in == 0))
+            def _():
+                for spot in range(nc - 2, half_line - 1, -1):
+                    emit(conv, spot, True, 0, frames)
+
+            @pl.when((i < blocks) & (place_in > 0))
+            def _():
+                emit(conv, nc - 1, True, i * fb, fb)
+
+            return 0
+
+        lax.fori_loop(0, half * blocks, far_block, 0)
+        lax.fori_loop(0, (ngroups - half) * blocks, near_block, 0)
+
+        for spot in range(half_line - 1):
+            @pl.when(place_in > spot)
+            def _():
+                emit(conv, spot, False, 0, frames)
+
+        for spot in range(nc - 2, 0, -1):
+            @pl.when((place_in > 0) if spot >= half_line else (place_in < spot))
+            def _():
+                emit(conv, spot, True, 0, frames)
 
         meanwhile()
 
         def body(m, sums):
-            for way, condition in ((0, c > 0), (1, c < nc - 1)):
+            for way, condition in ((1, border == 0), (0, place_in > 0)):
                 @pl.when(condition)
                 def _():
-                    rs_copy(conv, c, m, way).wait_recv()
-                    part[c, rows_of(m)] = part[c, rows_of(m)] + rcv[conv, way, c, m].astype(F32)
+                    take(conv, c, m, way)
+
+            take(conv, c, m, 2)
             v = (part[c, rows_of(m)] + vecs[bias]).astype(BF16)
             xv[m] = v.reshape(band, width, ch)
             finish(m)
@@ -340,7 +338,9 @@
     loads[2].start()
     set_moments(0, sums_of(xv[...].reshape(cells, ch)))
     pl.semaphore_wait(
-        barrier, nr - 1 + jnp.where(c > 0, 1, 0) + jnp.where(c < nc - 1, 1, 0)
+        barrier,
+        nr - 1 + jnp.where(c > 0, 1, 0) + jnp.where(c < nc - 1, 1, 0)
+        + (1 - border) + border * (nc - half_line - 1),
     )
     for o in range(1, nr):
         moment_copy(0, o).start()
@@ -383,14 +383,13 @@
         for o in range(1, nr):
             moment_copy(conv, o).wait_send()
         for d in range(nc):
-            for way, condition in ((0, c < d), (1, c > d)):
-                @pl.when(condition)
-                def _():
-                    def body(m, _):
-                        rs_copy(conv, d, m, way).wait_send()
-                        return 0
-
-                    lax.fori_loop(0, frames, body, 0)
+            @pl.when(c != d)
+            def _():
+                def body(m, _):
+                    rs_copy(conv, d, m, 0, d).wait_send()
+                    return 0
+
+                lax.fori_loop(0, frames, body, 0)
 
 
 def hand_over(a_hbm, b_hbm, c_hbm, d_hbm, a_held, b_held, in_sem, out_sem):
@@ -441,7 +440,7 @@
             pltpu.VMEM((2, nr, 8, ch), F32),
             pltpu.VMEM((nc, cells, ch), F32),
             pltpu.VMEM((2, nc, frames, band * width, ch), BF16),
-            pltpu.VMEM((2, 2, nc, frames, band * width, ch), BF16),
+            pltpu.VMEM((2, 3, nc, frames, band * width, ch), BF16),
             pltpu.SemaphoreType.DMA((11,)),
             pltpu.SemaphoreType.DMA((frames + 1,)),
             pltpu.SemaphoreType.DMA((2, nr)),
@@ -449,7 +448,7 @@
             pltpu.SemaphoreType.DMA((2, 2, 2)),
             pltpu.SemaphoreType.DMA((2, 2, 2)),
             pltpu.SemaphoreType.DMA((2, nc, frames)),
-            pltpu.SemaphoreType.DMA((2, 2, nc, frames)),
+            pltpu.SemaphoreType.DMA((2, 3, nc, frames)),
         ],
         compiler_params=pltpu.CompilerParams(
             collective_id=0, has_side_effects=True, vmem_limit_bytes=63 * 1024 * 1024

time: 45.8 us -> 46.1 us (level)
  Pallas kernels: 44.5 us -> 45.3 us
    pallas_call x1, Pallas kernels: 42.9 us -> 43.6 us  [local(): pl.pallas_call(functools.partial(kernel, nr, nc, channels), out_shape=(ja...]
where the time goes in v5:
time: 46.1 us; the launch traced here: 45.9 us
  Pallas kernels  45.3 us (98%)
  between operations  0.64 us (1%)
    pallas_call x1, Pallas kernels, local(): pl.pallas_call(functools.partial(kernel, nr, nc, channels), out_shape=(ja...  43.6 us
    pallas_call x1, Pallas kernels, local(): pl.pallas_call(hand_over, out_shape=(jax.ShapeDtypeStruct(decoded.shape,...  1.64 us

profile of v5, /device:TPU:0, one launch (start us, length us, event | category | flops | bytes accessed | tf_op | source)
XLA Modules:
  0.0 45.9 jit_solution(4814388800333513042)
XLA Ops:
  0.6 43.6 %shard_map.122 = (bf16[4,2,96,128]{3,2,1,0:T(8,128)(2,1)}, bf16[2,2,96,128]{3,2,1,0:T(8,128)(2,1)}) custom-call(bf16[4,2,96,128]{3,2,1,0:T(8,128)(2,1)} %bitcast.15, bf16[2,2,96,128]{3,2,1,0:T(8,128)(2,1)} %bitcast.17, f32[1,128]{1,0:T(1,128)} %bitcast.20, f32[1,128]{1,0:T(1,128)} %bitcast.21, bf16[3456,512]{1,0:T(8,128)(2,1)} %bitcast.13, ...), custom_call_target="tpu_custom_call" | custom-call | flops 5435817984 | bytes 7077888 | tf_op jit(solution)/shard_map/pallas_call | solution.py:424
  44.3 1.6 %shard_map.123 = (bf16[4,2,96,128]{3,2,1,0:T(8,128)(2,1)}, bf16[2,2,96,128]{3,2,1,0:T(8,128)(2,1)}) custom-call(bf16[4,2,96,128]{3,2,1,0:T(8,128)(2,1)} %get-tuple-element.6.a_hbm, bf16[2,2,96,128]{3,2,1,0:T(8,128)(2,1)} %get-tuple-element.7.b_hbm), custom_call_target="tpu_custom_call" | custom-call | tf_op jit(solution)/shard_map/pallas_call | solution.py:465

commit v6 on v5

--- a/solution.py
+++ b/solution.py
@@ -179,13 +179,14 @@
 
     def place_current(src, conv, gain, shift, stats, sides, first, keep=False):
         average, inverse = stats
-        gain, shift = vecs[gain], vecs[shift]
+        slope = 0.5 * inverse * vecs[gain]
+        level = 0.5 * vecs[shift] - average * slope
 
         def body(f, _):
             for p in sides:
                 v = row_of(src, conv, f + past, f, p).astype(F32)
-                u = ((v - average) * inverse) * gain + shift
-                v = (u / (1.0 + jnp.exp(-u))).astype(BF16)
+                u = v * slope + level
+                v = (u + u * jnp.tanh(u)).astype(BF16)
                 if keep:
                     @pl.when(f >= frames - past)
                     def _():
@@ -205,13 +206,10 @@
 
     def multiply(conv, g, m):
         cols = pl.ds(pl.multiple_of(g * gw, gw), gw)
-        acc = None
-        for dt in range(3):
-            lhs = x9[conv, pl.ds(m * fb + dt, fb)].reshape(mb, taps)
-            prod = jnp.dot(
-                lhs, w[conv, dt * taps : (dt + 1) * taps, cols], preferred_element_type=F32
-            )
-            acc = prod if acc is None else acc + prod
+        lhs = jnp.concatenate(
+            [x9[conv, pl.ds(m * fb + dt, fb)].reshape(mb, taps) for dt in range(3)], axis=1
+        )
+        acc = jnp.dot(lhs, w[conv, :, cols], preferred_element_type=F32)
         rows = pl.ds(pl.multiple_of(m * mb, mb), mb)
         for q in range(each):
             part[g * each + q, rows] = acc[:, q * ch : (q + 1) * ch]

time: 46.1 us -> 45.7 us (level)
  no operation moved by 1% of the time
where the time goes in v6:
time: 45.7 us; the launch traced here: 45.5 us
  Pallas kernels  44.9 us (98%)
  between operations  0.64 us (1%)
    pallas_call x1, Pallas kernels, local(): pl.pallas_call(functools.partial(kernel, nr, nc, channels), out_shape=(ja...  43.2 us
    pallas_call x1, Pallas kernels, local(): pl.pallas_call(hand_over, out_shape=(jax.ShapeDtypeStruct(decoded.shape,...  1.64 us

profile of v6, /device:TPU:0, one launch (start us, length us, event | category | flops | bytes accessed | tf_op | source)
XLA Modules:
  0.0 45.5 jit_solution(14244639223229619800)
XLA Ops:
  0.6 43.2 %shard_map.122 = (bf16[4,2,96,128]{3,2,1,0:T(8,128)(2,1)}, bf16[2,2,96,128]{3,2,1,0:T(8,128)(2,1)}) custom-call(bf16[4,2,96,128]{3,2,1,0:T(8,128)(2,1)} %bitcast.15, bf16[2,2,96,128]{3,2,1,0:T(8,128)(2,1)} %bitcast.17, f32[1,128]{1,0:T(1,128)} %bitcast.20, f32[1,128]{1,0:T(1,128)} %bitcast.21, bf16[3456,512]{1,0:T(8,128)(2,1)} %bitcast.13, ...), custom_call_target="tpu_custom_call" | custom-call | flops 5435817984 | bytes 7077888 | tf_op jit(solution)/shard_map/pallas_call | solution.py:422
  43.9 1.6 %shard_map.123 = (bf16[4,2,96,128]{3,2,1,0:T(8,128)(2,1)}, bf16[2,2,96,128]{3,2,1,0:T(8,128)(2,1)}) custom-call(bf16[4,2,96,128]{3,2,1,0:T(8,128)(2,1)} %get-tuple-element.6.a_hbm, bf16[2,2,96,128]{3,2,1,0:T(8,128)(2,1)} %get-tuple-element.7.b_hbm), custom_call_target="tpu_custom_call" | custom-call | tf_op jit(solution)/shard_map/pallas_call | solution.py:463

commit v7 on v6

--- a/solution.py
+++ b/solution.py
@@ -290,7 +290,11 @@
                 emit(conv, spot, False, 0, frames)
 
         for spot in range(nc - 2, 0, -1):
-            @pl.when((place_in > 0) if spot >= half_line else (place_in < spot))
+            ready = (place_in > 0) if spot >= half_line else (place_in < spot)
+            if conv == 0:
+                ready = ready & (place_in > 0)
+
+            @pl.when(ready)
             def _():
                 emit(conv, spot, True, 0, frames)
 
@@ -363,6 +367,12 @@
     for o in range(1, nr):
         moment_copy(1, o).start()
     halo_start(xv, 1, 1)
+
+    @pl.when(place_in == 0)
+    def _():
+        for spot in range(half_line - 1, 0, -1):
+            emit(0, spot, True, 0, frames)
+
     ready = prepare(1, 3, 4, statistics(1), True)
     loads[4].wait()
 

time: 45.7 us -> 50.1 us (1.096)
  Pallas kernels: 44.9 us -> 49.2 us
    pallas_call x1, Pallas kernels: 43.2 us -> 47.5 us  [local(): pl.pallas_call(functools.partial(kernel, nr, nc, channels), out_shape=(ja...]
where the time goes in v7:
time: 50.1 us; the launch traced here: 49.8 us
  Pallas kernels  49.2 us (98%)
  between operations  0.64 us (1%)
    pallas_call x1, Pallas kernels, local(): pl.pallas_call(functools.partial(kernel, nr, nc, channels), out_shape=(ja...  47.5 us
    pallas_call x1, Pallas kernels, local(): pl.pallas_call(hand_over, out_shape=(jax.ShapeDtypeStruct(decoded.shape,...  1.64 us

profile of v7, /device:TPU:0, one launch (start us, length us, event | category | flops | bytes accessed | tf_op | source)
XLA Modules:
  0.0 49.8 jit_solution(6298461150792601297)
XLA Ops:
  0.6 47.5 %shard_map.122 = (bf16[4,2,96,128]{3,2,1,0:T(8,128)(2,1)}, bf16[2,2,96,128]{3,2,1,0:T(8,128)(2,1)}) custom-call(bf16[4,2,96,128]{3,2,1,0:T(8,128)(2,1)} %bitcast.15, bf16[2,2,96,128]{3,2,1,0:T(8,128)(2,1)} %bitcast.17, f32[1,128]{1,0:T(1,128)} %bitcast.20, f32[1,128]{1,0:T(1,128)} %bitcast.21, bf16[3456,512]{1,0:T(8,128)(2,1)} %bitcast.13, ...), custom_call_target="tpu_custom_call" | custom-call | flops 5435817984 | bytes 7077888 | tf_op jit(solution)/shard_map/pallas_call | solution.py:432
  48.2 1.6 %shard_map.123 = (bf16[4,2,96,128]{3,2,1,0:T(8,128)(2,1)}, bf16[2,2,96,128]{3,2,1,0:T(8,128)(2,1)}) custom-call(bf16[4,2,96,128]{3,2,1,0:T(8,128)(2,1)} %get-tuple-element.6.a_hbm, bf16[2,2,96,128]{3,2,1,0:T(8,128)(2,1)} %get-tuple-element.7.b_hbm), custom_call_target="tpu_custom_call" | custom-call | tf_op jit(solution)/shard_map/pallas_call | solution.py:473
